TPU v7x, 32 devices: a whole 2x2x4 slice. The times are simulated.
32 devices in a mesh: groups: 2 (over x), wide: 16 (over z, y, core).
Axes of the slice: x: 2, y: 2, z: 4, core: 2. Of those that a mesh axis runs over, the one named last changes fastest.
Arguments:
- frames: bfloat16 [2048, 3072], P(('groups', 'wide')), parts along dimension 0, may hold values from -6 to 6
- latent_len: int32 [64], P('groups'), parts along dimension 0, may hold values from 1 to 9, as said below
- reader: int32 [64], P('groups'), parts along dimension 0, may hold values from 0 to 15, as said below
- owner: int32 [64], P('groups'), parts along dimension 0, may hold values from 0 to 15, as said below
- w_in: bfloat16 [128, 81], replicated, may hold values from -0.625 to 0.625
- b_in: float32 [128], replicated, may hold values from -3 to 3
- g_in: float32 [128], replicated, may hold values from 0.25 to 1.75
- w_down: bfloat16 [128, 512], replicated, may hold values from -0.25 to 0.25
- b_down: float32 [128], replicated, may hold values from -3 to 3
- g_down: float32 [128], replicated, may hold values from 0.25 to 1.75
- w_head: bfloat16 [16, 8192], replicated, may hold values from -0.0625 to 0.0625
- b_head: float32 [16], replicated, may hold values from -3 to 3
Outputs:
- latents: bfloat16 [576, 256], P(('groups', 'wide')), parts along dimension 0
There are 2 independent parts, one for each index of `groups`. A program takes and returns all parts, laid end to end along the dimension named above; an argument that names none is the same for every part. Nothing has to cross between parts.
Inputs may be any that keep to these rules, and one draw needn't show every extreme that they name: `latent_len`: all entries sum to 144. Every reader holds exactly two clips, with at most 16 latent frames between them; some reader holds exactly 16. An owner holds at most four clips and at most 18 latent frames; some owner holds four clips with 18 latent frames.
All inputs are finite; a program needn't handle non-finite values.
Results may differ from a plain program's by a relative error of at most 0.0046.
Values may be sent and summed in bfloat16 or wider, within the bound.
A program may use at most 256 MiB of HBM per device.

v0:
```python
import jax
import jax.numpy as jnp
from jax import lax
from jax.sharding import PartitionSpec as P

PIX = 32


epsilon = 1e-06


def clip_tables(latent_len, reader, owner):
    clip_count = latent_len.shape[0]
    clip_range = jnp.arange(clip_count, dtype=jnp.int32)
    earlier = clip_range[None, :] < clip_range[:, None]
    frame_len = 4 * latent_len - 3
    same_reader = reader[None, :] == reader[:, None]
    same_owner = owner[None, :] == owner[:, None]
    read_off = jnp.sum(jnp.where(earlier & same_reader, frame_len[None, :], 0), axis=1)
    own_off = jnp.sum(jnp.where(earlier & same_owner, latent_len[None, :], 0), axis=1)
    order_key = reader * clip_count + clip_range
    before = order_key[None, :] < order_key[:, None]
    deal_start = jnp.sum(jnp.where(before, latent_len[None, :], 0), axis=1)
    return (read_off, own_off, deal_start)


def find_clip(group_ids, deal_start, latent_len):
    clip_range = jnp.arange(latent_len.shape[0], dtype=jnp.int32)
    inside = (deal_start[None, :] <= group_ids[:, None]) & (
        group_ids[:, None] < (deal_start + latent_len)[None, :]
    )
    clip_ids = jnp.sum(jnp.where(inside, clip_range[None, :], 0), axis=1)
    present = jnp.any(inside, axis=1)
    latent_idx = group_ids - deal_start[clip_ids]
    return (clip_ids, latent_idx, present)


def frame_index(latent_idx):
    slot_ids = jnp.arange(6, dtype=jnp.int32)
    later = 4 * latent_idx[:, None] - 5 + slot_ids[None, :]
    opening = jnp.broadcast_to(slot_ids[None, :] - 5, later.shape)
    return jnp.where(latent_idx[:, None] > 0, later, opening)


def channel_norm_silu(values, gain_vec):
    mean_square = jnp.mean(values * values, axis=2, keepdims=True)
    return jax.nn.silu(values * lax.rsqrt(mean_square + epsilon) * gain_vec[None, None, :, None])


def encode_batch(blocks, opening, weights):
    w_in, b_in, g_in, w_down, b_down, g_down, w_head, b_head = weights
    channels = w_in.shape[0]
    count = blocks.shape[0]
    side = PIX
    quarter = side // 8
    picture = blocks.reshape(count, 6, 3, side, side)
    padded = jnp.pad(picture, ((0, 0), (0, 0), (0, 0), (1, 1), (1, 1)))
    taps = jnp.stack(
        [
            padded[:, :, :, row_off : row_off + side, col_off : col_off + side]
            for row_off in range(3)
            for col_off in range(3)
        ],
        axis=2,
    )
    taps = taps.reshape(count, 6, 27, quarter, 4, 2, quarter, 4, 2)
    taps = taps.transpose(0, 1, 2, 5, 8, 4, 7, 3, 6).reshape(count, 6, 27, side * side)
    columns = jnp.stack(
        [taps[:, slot : slot + 3].reshape(count, 81, side * side) for slot in range(4)], axis=1
    )
    convolved = (
        jnp.einsum("ck,gskp->gscp", w_in, columns, preferred_element_type=jnp.float32)
        + b_in[None, None, :, None]
    )
    full_res = channel_norm_silu(convolved, g_in).astype(jnp.bfloat16)
    merged = full_res.reshape(count, 4, 4 * channels, side * side // 4)
    lowered = (
        jnp.einsum("dm,gsmq->gsdq", w_down, merged, preferred_element_type=jnp.float32)
        + b_down[None, None, :, None]
    )
    reduced = channel_norm_silu(lowered, g_down).astype(jnp.bfloat16)
    early_slot = jnp.arange(4, dtype=jnp.int32) < 3
    blank = opening[:, None, None, None] & early_slot[None, :, None, None]
    reduced = jnp.where(blank, jnp.zeros((), jnp.bfloat16), reduced)
    stacked = reduced.reshape(count, 64 * channels, quarter * quarter)
    latent = (
        jnp.einsum("lm,gmq->glq", w_head, stacked, preferred_element_type=jnp.float32)
        + b_head[None, :, None]
    )
    return latent.reshape(count, -1).astype(jnp.bfloat16)


def collect_blocks(frames, group_ids, present, deal_start, latent_len, read_off):
    clip_ids, latent_idx, _ = find_clip(group_ids, deal_start, latent_len)
    frame_ids = frame_index(latent_idx)
    live = (frame_ids >= 0) & present[:, None]
    row_ids = read_off[clip_ids][:, None] + jnp.maximum(frame_ids, 0)
    return jnp.where(live[:, :, None], frames[row_ids], jnp.zeros((), frames.dtype))


def shards(
    frames, latent_len, reader, owner, w_in, b_in, g_in, w_down, b_down, g_down, w_head, b_head
):
    weights = (w_in, b_in, g_in, w_down, b_down, g_down, w_head, b_head)
    wide_n = lax.axis_size("wide")
    own_index = lax.axis_index("wide")
    read_rows = frames.shape[0]
    most_read = read_rows // 4
    per_device = (most_read + 2) // 2
    own_rows = 2 * per_device
    read_off, own_off, deal_start = clip_tables(latent_len, reader, owner)
    device_ids = jnp.arange(wide_n, dtype=jnp.int32)
    below = reader[None, :] < device_ids[:, None]
    first_group = jnp.sum(jnp.where(below, latent_len[None, :], 0), axis=1)
    group_count = jnp.sum(
        jnp.where(reader[None, :] == device_ids[:, None], latent_len[None, :], 0), axis=1
    )
    my_first = first_group[own_index]
    my_count = group_count[own_index]
    target_groups = my_first + (device_ids - my_first) % wide_n
    target_present = target_groups - my_first < my_count
    outgoing = collect_blocks(
        frames, target_groups, target_present, deal_start, latent_len, read_off
    )
    incoming = lax.all_to_all(outgoing, "wide", split_axis=0, concat_axis=0, tiled=True)
    made_groups = own_index + jnp.arange(per_device, dtype=jnp.int32) * wide_n
    made_clip, made_step, _ = find_clip(made_groups, deal_start, latent_len)
    blocks = incoming[reader[made_clip]]
    encoded = encode_batch(blocks, made_step == 0, weights)
    slot_ids = jnp.arange(own_rows, dtype=jnp.int32)
    clip_range = jnp.arange(latent_len.shape[0], dtype=jnp.int32)
    inside = (
        (owner == own_index)[None, :]
        & (own_off[None, :] <= slot_ids[:, None])
        & (slot_ids[:, None] < (own_off + latent_len)[None, :])
    )
    slot_clip = jnp.sum(jnp.where(inside, clip_range[None, :], 0), axis=1)
    slot_live = jnp.any(inside, axis=1)
    slot_group = deal_start[slot_clip] + slot_ids - own_off[slot_clip]
    producer = slot_group % wide_n
    made_row = slot_group // wide_n
    source_row = producer * per_device + made_row
    shard_rows = lax.all_gather(encoded, "wide", axis=0, tiled=True)
    width = shard_rows.shape[0]
    pick_matrix = (
        (source_row[:, None] == jnp.arange(width, dtype=jnp.int32)[None, :]) & slot_live[:, None]
    ).astype(jnp.bfloat16)
    gathered = jnp.dot(pick_matrix, shard_rows, preferred_element_type=jnp.float32)
    result = gathered.astype(jnp.bfloat16)
    return result


def solution(mesh):
    return jax.shard_map(
        shards,
        mesh=mesh,
        in_specs=(
            P(("groups", "wide"), None),
            P("groups"),
            P("groups"),
            P("groups"),
            P(),
            P(),
            P(),
            P(),
            P(),
            P(),
            P(),
            P(),
        ),
        out_specs=P(("groups", "wide"), None),
        check_vma=False,
    )
```

profile of v0, /device:TPU:0, one launch (start us, length us, event | category | flops | bytes accessed | tf_op | source)
XLA Modules:
  0.0 318.7 jit_solution(2204087388025711747)
XLA Ops:
  0.0 0.7 iota_add_fusion.1
  0.7 0.8 select_reduce_fusion.4
  1.5 0.6 dynamic_slice.6
  2.1 0.7 dynamic_slice.7
  2.8 0.7 broadcast_add_fusion
  3.4 0.9 select_reduce_fusion.1
  4.3 0.7 fusion.58
  5.0 0.9 select_reduce_fusion
  5.9 0.2 select_reduce_fusion.5
  6.1 0.7 gather_fusion.3
  6.8 0.7 gather_fusion.4
  7.4 0.7 multiply_add_fusion.1
  8.1 1.4 broadcast_compare_fusion
  9.5 0.1 fusion.47
  9.5 0.1 compare_select_fusion
  9.6 0.1 reshape.448
  9.7 0.0 copy-start.2
  9.7 0.9 gather_fusion.5
  10.7 0.2 reshape.447
  10.9 1.0 broadcast_select_fusion
  11.9 7.4 %all-to-all-start = ((bf16[16,6,3072]{2,1,0:T(8,128)(2,1)}), bf16[16,6,3072]{2,1,0:T(8,128)(2,1)S(1)}, u32[]{:S(2)}, u32[]{:S(2)}) async-start(bf16[16,6,3072]{2,1,0:T(8,128)(2,1)} %broadcast_select_fusion), calls=%async_computation | async-start | bytes 1572864 | tf_op jit(solution)/shard_map/all_to_all | solution.py:125
  19.3 0.2 select_reduce_fusion.7
  19.5 0.1 select_reduce_fusion.3
  19.7 0.7 gather_fusion.1
  20.4 0.7 gather_fusion
  21.1 0.7 gather_fusion.2
  21.7 0.7 gather_fusion.6
  22.4 0.1 fusion.48
  22.6 0.1 broadcast_and_fusion
  22.6 15.3 %all-to-all-done = bf16[16,6,3072]{2,1,0:T(8,128)(2,1)S(1)} async-done(((bf16[16,6,3072]{2,1,0:T(8,128)(2,1)}), bf16[16,6,3072]{2,1,0:T(8,128)(2,1)S(1)}, u32[]{:S(2)}, u32[]{:S(2)}) %all-to-all-start) | async-done | bytes 589856 | tf_op jit(solution)/shard_map/all_to_all | solution.py:125
  38.0 0.6 gather_fusion.7
  38.6 3.4 %copy.65 = bf16[9,6,3072]{0,2,1:T(8,128)(2,1)} copy(bf16[9,6,3072]{2,1,0:T(8,128)(2,1)S(1)} %gather_fusion.7) | data formatting | bytes 663552 | tf_op jit(solution)/shard_map/reshape | solution.py:56
  42.0 6.3 %fusion.13 = bf16[9,6,9,3,32,32]{0,5,4,3,2,1:T(8,128)(2,1)} fusion(bf16[9,6,3,32,32]{0,4,3,2,1:T(8,128)(2,1)} %bitcast.126), kind=kLoop, calls=%fused_computation.32 | loop fusion | bytes 5050368
  48.3 3.5 %fusion.15 = bf16[9,6,9,3,32,32]{0,5,4,3,2,1:T(8,128)(2,1)} fusion(bf16[9,6,9,3,32,32]{0,5,4,3,2,1:T(8,128)(2,1)} %fusion.13, bf16[9,6,3,32,32]{0,4,3,2,1:T(8,128)(2,1)S(1)} %bitcast.129), kind=kLoop, calls=%fused_computation.34 | loop fusion | bytes 5050368
  51.8 3.9 %fusion.17 = bf16[9,6,9,3,32,32]{0,5,4,3,2,1:T(8,128)(2,1)} fusion(bf16[9,6,9,3,32,32]{0,5,4,3,2,1:T(8,128)(2,1)} %fusion.15, bf16[9,6,3,32,32]{0,4,3,2,1:T(8,128)(2,1)S(1)} %bitcast.130), kind=kLoop, calls=%fused_computation.36 | loop fusion | bytes 5050368
  55.7 4.1 %fusion.19 = bf16[9,6,9,3,32,32]{0,5,4,3,2,1:T(8,128)(2,1)} fusion(bf16[9,6,9,3,32,32]{0,5,4,3,2,1:T(8,128)(2,1)} %fusion.17, bf16[9,6,3,32,32]{0,4,3,2,1:T(8,128)(2,1)S(1)} %bitcast.131), kind=kLoop, calls=%fused_computation.38 | loop fusion | bytes 5050368
  59.8 3.1 constant_dynamic-update-slice_fusion
  62.9 4.1 %fusion.21 = bf16[9,6,9,3,32,32]{0,5,4,3,2,1:T(8,128)(2,1)} fusion(bf16[9,6,9,3,32,32]{0,5,4,3,2,1:T(8,128)(2,1)} %constant_dynamic-update-slice_fusion, bf16[9,6,3,32,32]{0,4,3,2,1:T(8,128)(2,1)S(1)} %bitcast.133), kind=kLoop, calls=%fused_computation.40 | loop fusion | bytes 5050368
  67.0 4.2 %fusion.23 = bf16[9,6,9,3,32,32]{0,5,4,3,2,1:T(8,128)(2,1)} fusion(bf16[9,6,9,3,32,32]{0,5,4,3,2,1:T(8,128)(2,1)} %fusion.21, bf16[9,6,3,32,32]{0,4,3,2,1:T(8,128)(2,1)S(1)} %bitcast.134), kind=kLoop, calls=%fused_computation.42 | loop fusion | bytes 5050368
  71.2 3.8 %fusion.25 = bf16[9,6,9,3,32,32]{0,5,4,3,2,1:T(8,128)(2,1)} fusion(bf16[9,6,9,3,32,32]{0,5,4,3,2,1:T(8,128)(2,1)} %fusion.23, bf16[9,6,3,32,32]{0,4,3,2,1:T(8,128)(2,1)S(1)} %bitcast.135), kind=kLoop, calls=%fused_computation.44 | loop fusion | bytes 5050368
  74.9 4.0 %fusion.27 = bf16[9,6,9,3,32,32]{0,5,4,3,2,1:T(8,128)(2,1)} fusion(bf16[9,6,9,3,32,32]{0,5,4,3,2,1:T(8,128)(2,1)} %fusion.25, bf16[9,6,3,32,32]{0,4,3,2,1:T(8,128)(2,1)S(1)} %bitcast.136), kind=kLoop, calls=%fused_computation.46 | loop fusion | bytes 5050368 | tf_op jit(solution)/shard_map/stack | solution.py:58
  79.0 101.5 %copy.55 = bf16[9,6,27,2,2,4,4,4,4]{2,8,7,6,5,4,3,1,0:T(4,128)(2,1)} copy(bf16[9,6,27,2,2,4,4,4,4]{0,4,6,8,3,5,7,2,1:T(2,128)(2,1)} %bitcast.138) | data formatting | bytes 5971968 | tf_op jit(solution)/shard_map/transpose | solution.py:67
  180.4 21.2 %fusion.57 = (bf16[9,3,27,1024]{2,3,1,0:T(8,128)(2,1)}, bf16[9,3,27,1024]{2,3,1,0:T(8,128)(2,1)}, bf16[9,3,27,1024]{2,3,1,0:T(8,128)(2,1)}, bf16[9,3,27,1024]{2,3,1,0:T(8,128)(2,1)}) fusion(bf16[9,6,27,1024]{2,3,1,0:T(8,128)(2,1)} %bitcast.137), kind=kLoop, calls=%fused_computation.129 | loop fusion | bytes 11943936 | tf_op jit(solution)/shard_map/slice | solution.py:69
  201.6 5.7 %copy.56 = bf16[9,3,27,1024]{3,2,1,0:T(8,128)(2,1)S(1)} copy(bf16[9,3,27,1024]{2,3,1,0:T(8,128)(2,1)} %get-tuple-element.9) | data formatting | bytes 2985984 | tf_op jit(solution)/shard_map/slice | solution.py:69
  207.4 1.9 stack_reshape.12
  209.3 5.7 %copy.59 = bf16[9,3,27,1024]{3,2,1,0:T(8,128)(2,1)S(1)} copy(bf16[9,3,27,1024]{2,3,1,0:T(8,128)(2,1)} %get-tuple-element.10) | data formatting | bytes 2985984 | tf_op jit(solution)/shard_map/slice | solution.py:69
  215.0 1.9 stack_reshape.15
  216.9 5.7 %copy.58 = bf16[9,3,27,1024]{3,2,1,0:T(8,128)(2,1)S(1)} copy(bf16[9,3,27,1024]{2,3,1,0:T(8,128)(2,1)} %get-tuple-element.11) | data formatting | bytes 2985984 | tf_op jit(solution)/shard_map/slice | solution.py:69
  222.6 1.9 stack_reshape.14
  224.5 5.7 %copy.57 = bf16[9,3,27,1024]{3,2,1,0:T(8,128)(2,1)S(1)} copy(bf16[9,3,27,1024]{2,3,1,0:T(8,128)(2,1)} %get-tuple-element.12) | data formatting | bytes 2985984 | tf_op jit(solution)/shard_map/slice | solution.py:69
  230.3 1.9 stack_reshape.13
  232.2 6.2 %multiply_reduce_fusion = (f32[9,4,1024]{2,1,0:T(4,128)S(1)}, f32[9,4,1024,128]{2,3,1,0:T(8,128)S(1)}) fusion(f32[128]{0:T(128)S(1)} %copy-done.9, bf16[128,81]{0,1:T(8,128)(2,1)S(1)} %copy-done.11, bf16[9,1,81,1024]{3,2,1,0:T(8,128)(2,1)} %stack_reshape.15, bf16[9,1,81,1024]{3,2,1,0:T(8,128)(2,1)} %stack_reshape.14, ...), kind=kOutput, calls=%fused_computation.13 | convolution fusion | flops 787488768 | bytes 25015040 | tf_op jit(solution)/shard_map/ck,gskp->gscp/dot_general | solution.py:72
  238.3 0.1 add_rsqrt_fusion
  238.4 7.6 %fusion.3 = bf16[9,4,128,1024]{3,2,1,0:T(8,128)(2,1)} fusion(f32[9,4,1024,128]{2,3,1,0:T(8,128)S(1)} %get-tuple-element.17, f32[128]{0:T(128)S(1)} %copy-done.10, f32[9,4,1024]{2,1,0:T(4,128)S(1)} %add_rsqrt_fusion, f32[128]{0:T(128)S(1)} %copy-done.9), kind=kLoop, calls=%fused_computation.14 | loop fusion | flops 37748736 | bytes 28460032 | tf_op jit(solution)/shard_map/convert_element_type | solution.py:75
  246.0 15.6 %reshape.404 = bf16[9,4,512,256]{3,2,1,0:T(8,128)(2,1)} reshape(bf16[9,4,128,1024]{3,2,1,0:T(8,128)(2,1)} %fusion.3) | data formatting | bytes 18874368 | tf_op jit(solution)/shard_map/reshape | solution.py:76
  261.6 5.1 %multiply_reduce_fusion.1 = (f32[9,4,256]{2,1,0:T(4,128)S(1)}, f32[9,4,256,128]{2,3,1,0:T(8,128)S(1)}) fusion(f32[128]{0:T(128)S(1)} %copy-done.6, bf16[9,4,512,256]{3,2,1,0:T(8,128)(2,1)} %reshape.404, bf16[128,512]{1,0:T(8,128)(2,1)S(1)} %copy-done.4), kind=kOutput, calls=%fused_computation.52 | convolution fusion | flops 1211489280 | bytes 14324224 | tf_op jit(solution)/shard_map/dm,gsmq->gsdq/dot_general | solution.py:78
  266.7 1.7 fusion.32
  268.5 0.0 copy-start.5
  268.5 16.1 %reshape.405 = bf16[9,8192,16]{2,1,0:T(8,128)(2,1)} reshape(bf16[9,4,128,256]{3,2,1,0:T(8,128)(2,1)S(1)} %fusion.32) | data formatting | bytes 4718592 | tf_op jit(solution)/shard_map/reshape | solution.py:85
  284.6 11.5 %fusion.34 = bf16[9,16,16]{1,2,0:T(8,128)(2,1)S(1)} fusion(bf16[9,8192,16]{2,1,0:T(8,128)(2,1)} %reshape.405, bf16[16,8192]{1,0:T(8,128)(2,1)S(1)} %copy-done.3, f32[16]{0:T(128)S(1)} %copy-done.5), kind=kOutput, calls=%fused_computation.57 | convolution fusion | flops 37753344 | bytes 2626112 | tf_op jit(solution)/shard_map/lm,gmq->glq/dot_general | solution.py:87
  296.1 0.1 copy.61
  296.2 0.1 reshape.471
  296.3 21.6 %all-gather = bf16[16,9,256]{2,1,0:T(8,128)(2,1)S(1)} all-gather(bf16[1,9,256]{2,1,0:T(8,128)(2,1)S(1)} %reshape.471), channel_id=1, replica_groups=mesh['groups'=2,'wide'=16] {'wide'}, dimensions={0}, use_global_device_ids=true | all-gather | bytes 78336 | tf_op jit(solution)/shard_map/all_gather | solution.py:143
  317.9 0.8 convolution_convert_fusion
  (43 shorter events, 0.2 us)
Async XLA Ops:
  0.0 9.7 %copy-start = (bf16[64,3072]{1,0:T(8,128)(2,1)S(1)}, bf16[64,3072]{1,0:T(8,128)(2,1)}, u32[]{:S(2)}) copy-start(bf16[64,3072]{1,0:T(8,128)(2,1)} %param.12) | copy-start | bytes 1179652
  0.0 19.3 %copy-start.7 = (s32[32]{0:T(128)S(1)}, s32[32]{0:T(128)}, u32[]{:S(2)}) copy-start(s32[32]{0:T(128)} %param.15) | copy-start | bytes 388
  9.7 12.0 %copy-start.2 = (s32[32]{0:T(128)S(1)}, s32[32]{0:T(128)}, u32[]{:S(2)}) copy-start(s32[32]{0:T(128)} %param.14) | copy-start | bytes 388
  11.9 26.1 %all-to-all-start = ((bf16[16,6,3072]{2,1,0:T(8,128)(2,1)}), bf16[16,6,3072]{2,1,0:T(8,128)(2,1)S(1)}, u32[]{:S(2)}, u32[]{:S(2)}) async-start(bf16[16,6,3072]{2,1,0:T(8,128)(2,1)} %broadcast_select_fusion), calls=%async_computation | async-start | bytes 1572864 | tf_op jit(solution)/shard_map/all_to_all | solution.py:125
  42.0 6.3 %slice-start = ((s8[4718592]{0:T(1024)(128)(4,1)}), s8[4194304]{0:T(1024)(128)(4,1)S(1)}, s32[]{:S(2)}) async-start(s8[4718592]{0:T(1024)(128)(4,1)} %bitcast.127), calls=%async_computation.1 | async-start | bytes 8388608
  42.0 6.3 %slice-start.1 = ((s8[4718592]{0:T(1024)(128)(4,1)}), s8[524288]{0:T(1024)(128)(4,1)S(1)}, s32[]{:S(2)}) async-start(s8[4718592]{0:T(1024)(128)(4,1)} %bitcast.127), calls=%async_computation.2 | async-start | bytes 1048576
  224.5 7.6 %copy-start.9 = (f32[128]{0:T(128)S(1)}, f32[128]{0:T(128)}, u32[]{:S(2)}) copy-start(f32[128]{0:T(128)} %param.17) | copy-start | bytes 1540
  224.5 7.6 %copy-start.11 = (bf16[128,81]{0,1:T(8,128)(2,1)S(1)}, bf16[128,81]{0,1:T(8,128)(2,1)}, u32[]{:S(2)}) copy-start(bf16[128,81]{0,1:T(8,128)(2,1)} %param.16) | copy-start | bytes 62212
  232.2 6.2 %copy-start.10 = (f32[128]{0:T(128)S(1)}, f32[128]{0:T(128)}, u32[]{:S(2)}) copy-start(f32[128]{0:T(128)} %param.18) | copy-start | bytes 1540
  246.0 15.6 %copy-start.4 = (bf16[128,512]{1,0:T(8,128)(2,1)S(1)}, bf16[128,512]{1,0:T(8,128)(2,1)}, u32[]{:S(2)}) copy-start(bf16[128,512]{1,0:T(8,128)(2,1)} %param.19) | copy-start | bytes 393220
  246.0 15.6 %copy-start.6 = (f32[128]{0:T(128)S(1)}, f32[128]{0:T(128)}, u32[]{:S(2)}) copy-start(f32[128]{0:T(128)} %param.20) | copy-start | bytes 1540
  261.6 5.2 %copy-start.8 = (f32[128]{0:T(128)S(1)}, f32[128]{0:T(128)}, u32[]{:S(2)}) copy-start(f32[128]{0:T(128)} %param.21) | copy-start | bytes 1540
  268.4 16.2 %copy-start.3 = (bf16[16,8192]{1,0:T(8,128)(2,1)S(1)}, bf16[16,8192]{1,0:T(8,128)(2,1)}, u32[]{:S(2)}) copy-start(bf16[16,8192]{1,0:T(8,128)(2,1)} %param.22) | copy-start | bytes 786436
  268.5 16.1 %copy-start.5 = (f32[16]{0:T(128)S(1)}, f32[16]{0:T(128)}, u32[]{:S(2)}) copy-start(f32[16]{0:T(128)} %param.23) | copy-start | bytes 196
  284.6 34.1 %copy-start.1 = (bf16[64,3072]{1,0:T(8,128)(2,1)S(1)}, bf16[64,3072]{1,0:T(8,128)(2,1)}, u32[]{:S(2)}) copy-start(bf16[64,3072]{1,0:T(8,128)(2,1)} %param.12) | copy-start | bytes 1179652
where the time goes:
time: 322 us; the launch traced here: 319 us
  local copies, waits for them, and re-layouts  233 us (72%)
  matrix products  23.5 us (7%)
  blocking collectives  21.6 us (7%)
  other arithmetic  17.9 us (6%)
  waiting for transfers between devices  15.3 us (5%)
  starting transfers between devices  7.39 us (2%)
    transpose x1, local copies, waits for them, and re-layouts, encode_batch(): taps.transpose(0, 1, 2, 5, 8, 4, 7, 3, 6).reshape(count, 6, 27, side * side)  101 us
    slice x5, local copies, waits for them, and re-layouts, encode_batch(): taps[:, slot:slot + 3].reshape(count, 81, side * side)  44.1 us
    unnamed x38, local copies, waits for them, and re-layouts  33.1 us
    all_gather x1, blocking collectives, shards(): shard_rows = lax.all_gather(encoded, 'wide', axis=0, tiled=True)  21.6 us
    reshape x1, local copies, waits for them, and re-layouts, encode_batch(): stacked = reduced.reshape(count, 64 * channels, quarter * quarter)  16.1 us
    reshape x1, local copies, waits for them, and re-layouts, encode_batch(): merged = full_res.reshape(count, 4, 4 * channels, side * side // 4)  15.6 us
    all_to_all x1, waiting for transfers between devices, shards(): lax.all_to_all(outgoing, 'wide', split_axis=0, concat_axis=0, tiled=True)  15.3 us
    dot_general x1, matrix products, encode_batch(): jnp.einsum('lm,gmq->glq', w_head, stacked, preferred_element_type=jnp.flo...  11.5 us
  transfers between devices with their start and end apart: 1, of which 1 were waited for; matrix products, arithmetic and copies ran while one was open for 1% of the time, Pallas kernels for 0%

commit v1 on v0

v1 whole, which is shorter than its diff:
```python
import functools

import jax
import jax.numpy as jnp
import numpy as np
from jax import lax
from jax.experimental import pallas as pl
from jax.experimental.pallas import tpu as pltpu
from jax.sharding import PartitionSpec as P

PIX = 32
EPS = 1e-6
WIN = 48
KDIM = 160
HALF = 256
MESH = pl.DeviceIdType.MESH


def window_table():
    table = np.zeros((512, 1024), np.float32)
    for py in range(2):
        for dx in range(4):
            for u in range(8):
                for v in range(16):
                    x = 2 * v + dx - 1
                    if 0 <= x < PIX:
                        table[(2 * u + py) * PIX + x, (py * 4 + dx) * 128 + u * 16 + v] = 1
    return table


def weight_table():
    table = np.zeros((81, 1024), np.float32)
    for py in range(2):
        for px in range(2):
            for t in range(3):
                for a in range(3):
                    for b in range(3):
                        for k in range(3):
                            col = t * WIN + ((a + py) * 4 + b + px) * 3 + k
                            table[t * 27 + (a * 3 + b) * 3 + k, (py * 2 + px) * 256 + col] = 1
    return table


def down_table():
    table = np.zeros((512, 512), np.float32)
    for c in range(128):
        for ab in range(4):
            table[4 * c + ab, ab * 128 + c] = 1
    return table


def place_table():
    px = np.arange(HALF)
    place = (px // 16 // 4) * 4 + (px % 16) // 4
    return (place[:, None] == (np.arange(256) % 16)[None, :]).astype(np.float32)


def iota(shape, axis):
    return lax.broadcasted_iota(jnp.int32, shape, axis)


def column(row):
    n = row.shape[1]
    same = iota((n, n), 0) == iota((n, n), 1)
    return jnp.sum(jnp.where(same, row, jnp.zeros((), row.dtype)), axis=1, keepdims=True)


def norm_silu(values, gain):
    mean_square = jnp.sum(values * values, axis=0, keepdims=True) * (1.0 / values.shape[0])
    half = (values * gain) * (0.5 * lax.rsqrt(mean_square + EPS))
    return (half + half * jnp.tanh(half)).astype(jnp.bfloat16)


def dot(a, b):
    return jnp.dot(a, b, preferred_element_type=jnp.float32)


def encode_kernel(
    len_ref, reader_ref, frames_ref, win_ref, bin_ref, gin_ref, wdown_ref, bdown_ref, gdown_ref,
    whead_ref, bhead_ref, wtab_ref, etab_ref, dtab_ref, ptab_ref,
    out_ref, windows, w2, wd, gin_s, gdown_s, bdown_s, parts,
):
    me = lax.axis_index("wide")
    read_rows = frames_ref.shape[0]
    most = read_rows // 4
    clips = len_ref.shape[0]
    first_len = jnp.int32(0)
    seen = jnp.int32(0)
    for c in range(clips):
        mine = reader_ref[c] == me
        first_len = jnp.where(mine & (seen == 0), len_ref[c], first_len)
        seen = seen + mine.astype(jnp.int32)
    second_at = 4 * first_len - 3

    stacked = jnp.concatenate(
        [
            frames_ref[:, k * 1024 + h * 512 : k * 1024 + (h + 1) * 512]
            for k in range(3)
            for h in range(2)
        ],
        axis=0,
    )
    planes = dot(stacked, wtab_ref[...])
    lane = iota((read_rows, HALF), 1)
    for k in range(3):
        for dx in range(4):
            plane = []
            for py in range(2):
                at = (py * 4 + dx) * 128
                plane.append(
                    jnp.concatenate(
                        [
                            planes[
                                (2 * k + h) * read_rows : (2 * k + h + 1) * read_rows,
                                at : at + 128,
                            ]
                            for h in range(2)
                        ],
                        axis=1,
                    )
                )
            above = jnp.where(lane < 16, 0.0, pltpu.roll(plane[1], 16, 1))
            below = jnp.where(lane >= HALF - 16, 0.0, pltpu.roll(plane[0], HALF - 16, 1))
            for dy, value in enumerate((above, plane[0], plane[1], below)):
                row = (dy * 4 + dx) * 3 + k
                for h in range(2):
                    windows[h, pl.ds(row, read_rows, stride=WIN), :] = value[
                        :, h * 128 : (h + 1) * 128
                    ]

    spread = dot(win_ref[...], etab_ref[...])
    bias = column(bin_ref[...])
    high = bias.astype(jnp.bfloat16).astype(jnp.float32)
    mid = (bias - high).astype(jnp.bfloat16).astype(jnp.float32)
    low = bias - high - mid
    kcol = iota((128, KDIM), 1)
    tail = jnp.where(kcol == 3 * WIN, high, 0.0)
    tail = tail + jnp.where(kcol == 3 * WIN + 1, mid, 0.0)
    tail = tail + jnp.where(kcol == 3 * WIN + 2, low, 0.0)
    for ab in range(4):
        w2[ab * 128 : (ab + 1) * 128, :] = (
            spread[:, ab * 256 : ab * 256 + KDIM] + tail
        ).astype(jnp.bfloat16)
    wd[...] = dot(wdown_ref[...], dtab_ref[...]).astype(jnp.bfloat16)
    gin_s[...] = jnp.broadcast_to(column(gin_ref[...]), gin_s.shape)
    gdown_s[...] = jnp.broadcast_to(column(gdown_ref[...]), gdown_s.shape)
    bdown_s[...] = jnp.broadcast_to(column(bdown_ref[...]), bdown_s.shape)

    ones = jnp.ones((KDIM - 3 * WIN, HALF), jnp.bfloat16)

    def load(slot, count):
        at = pl.multiple_of(slot * WIN, 8)
        halves = [windows[h, pl.ds(at, count * WIN), :] for h in range(2)]
        return jnp.concatenate(halves, axis=1).astype(jnp.bfloat16)

    def encode_frame(cols):
        cols = jnp.concatenate([cols, ones], axis=0)
        full = [
            norm_silu(dot(w2[ab * 128 : (ab + 1) * 128, :], cols), gin_s[...]) for ab in range(4)
        ]
        lowered = dot(wd[...], jnp.concatenate(full, axis=0)) + bdown_s[...]
        return norm_silu(lowered, gdown_s[...])

    pix = iota((16, HALF), 1)
    sub = ((pix // 16) % 4) * 4 + pix % 4

    def keep(spot, both):
        total = jnp.zeros((16, HALF), jnp.float32)
        for ab in range(16):
            total = total + jnp.where(sub == ab, both[ab * 16 : (ab + 1) * 16, :], 0.0)
        parts[pl.ds(pl.multiple_of(spot * 16, 16), 16), :] = total

    for spot, at in enumerate((jnp.int32(0), second_at)):
        cols = load(at, 1)
        cols = jnp.concatenate([jnp.zeros((2 * WIN, HALF), jnp.bfloat16), cols], axis=0)
        keep(spot, dot(whead_ref[:, 384:512], encode_frame(cols)))

    def group(n, carry):
        second = (n >= first_len - 1).astype(jnp.int32)
        step = n + 1 - second * (first_len - 1)
        base = second * second_at + 4 * step - 5
        base = jnp.minimum(base, read_rows - 6)
        head = load(jnp.maximum(base, 0), 1)
        head = head * (step > 1).astype(jnp.bfloat16)
        cols = jnp.concatenate([head, load(base + 1, 5)], axis=0)
        reduced = jnp.concatenate(
            [encode_frame(cols[s * WIN : (s + 3) * WIN, :]) for s in range(4)], axis=0
        )
        keep(n + 2, dot(whead_ref[...], reduced))
        return carry

    lax.fori_loop(0, most - 2, group, 0)

    rows = most * 16
    value = parts[...]
    top = value.astype(jnp.bfloat16)
    rest = (value - top.astype(jnp.float32)).astype(jnp.bfloat16)
    wide = dot(top, ptab_ref[...]) + dot(rest, ptab_ref[...])
    match = iota((rows, 256), 1) // 16 == iota((rows, 256), 0) % 16
    wide = jnp.where(match, wide, 0.0).reshape(most, 16, 256)
    bh = jnp.where(
        iota((16, 256), 1) // 16 == iota((16, 256), 0), column(bhead_ref[...]), 0.0
    )
    bh = jnp.sum(bh, axis=0, keepdims=True)
    result = jnp.sum(wide, axis=1) + bh
    out_rows = out_ref.shape[0]
    if out_rows > most:
        result = jnp.concatenate([result, jnp.zeros((out_rows - most, 256), jnp.float32)], axis=0)
    out_ref[...] = result.astype(jnp.bfloat16)


def spread_kernel(enc_ref, len_ref, reader_ref, owner_ref, out_ref, held, send_sem, recv_sem):
    me = lax.axis_index("wide")
    n, rows = held.shape[0], held.shape[1]
    barrier = pltpu.get_barrier_semaphore()
    for d in range(1, n):
        pl.semaphore_signal(
            barrier, inc=1, device_id={"wide": lax.rem(me + d, n)}, device_id_type=MESH
        )
    pl.semaphore_wait(barrier, n - 1)
    copies = []
    for d in range(1, n):
        copy = pltpu.make_async_remote_copy(
            src_ref=enc_ref,
            dst_ref=held.at[me],
            send_sem=send_sem.at[d],
            recv_sem=recv_sem.at[d],
            device_id={"wide": lax.rem(me + d, n)},
            device_id_type=MESH,
        )
        copy.start()
        copies.append(copy)
    held[me] = enc_ref[...]

    own_rows = out_ref.shape[0]
    clips = len_ref.shape[1]
    len_row, reader_row, owner_row = (
        ref[...].astype(jnp.float32) for ref in (len_ref, reader_ref, owner_ref)
    )
    len_col, reader_col, owner_col = column(len_row), column(reader_row), column(owner_row)
    earlier = iota((clips, clips), 1) < iota((clips, clips), 0)
    before_here = jnp.sum(
        jnp.where(earlier & (reader_row == reader_col), len_row, 0.0), axis=1, keepdims=True
    )
    own_off = jnp.sum(
        jnp.where(earlier & (owner_row == owner_col), len_row, 0.0), axis=1, keepdims=True
    )
    slot = iota((clips, 128), 1).astype(jnp.float32)
    step = slot - own_off
    inside = (owner_col == me.astype(jnp.float32)) & (step >= 0.0) & (step < len_col)
    late = before_here > 0.0
    opening = jnp.where(late, 1.0, 0.0)
    later = jnp.where(late, before_here, 1.0) + step
    source = reader_col * rows + jnp.where(step == 0.0, opening, later)
    picked = jnp.sum(jnp.where(inside, source + 1.0, 0.0), axis=0, keepdims=True) - 1.0
    pick = (iota((n * rows, 128), 0).astype(jnp.float32) == picked).astype(jnp.float32)
    pick = pick.T.astype(jnp.bfloat16)

    for copy in copies:
        copy.wait()
    result = dot(pick, held[...].reshape(n * rows, 256))
    out_ref[...] = result[:own_rows].astype(jnp.bfloat16)


def shards(
    frames, latent_len, reader, owner, w_in, b_in, g_in, w_down, b_down, g_down, w_head, b_head
):
    n = lax.axis_size("wide")
    read_rows = frames.shape[0]
    most = read_rows // 4
    held_rows = -(-most // 16) * 16
    own_rows = 2 * ((most + 2) // 2)
    heads = w_head.reshape(16, 512, 16).transpose(2, 0, 1).reshape(256, 512)
    vmem = pl.BlockSpec(memory_space=pltpu.VMEM)
    smem = pl.BlockSpec(memory_space=pltpu.SMEM)
    tables = [
        jnp.asarray(t, dtype=jnp.bfloat16)
        for t in (window_table(), weight_table(), down_table(), place_table())
    ]
    encoded = pl.pallas_call(
        encode_kernel,
        out_shape=jax.ShapeDtypeStruct((held_rows, 256), jnp.bfloat16),
        in_specs=[smem] * 2 + [vmem] * 13,
        out_specs=vmem,
        scratch_shapes=[
            pltpu.VMEM((2, read_rows * WIN, 128), jnp.float32),
            pltpu.VMEM((512, KDIM), jnp.bfloat16),
            pltpu.VMEM((128, 512), jnp.bfloat16),
            pltpu.VMEM((128, HALF), jnp.float32),
            pltpu.VMEM((128, HALF), jnp.float32),
            pltpu.VMEM((128, HALF), jnp.float32),
            pltpu.VMEM((most * 16, HALF), jnp.float32),
        ],
        compiler_params=pltpu.CompilerParams(vmem_limit_bytes=48 * 1024 * 1024),
        name="encode",
    )(
        latent_len, reader, frames, w_in, b_in[None, :], g_in[None, :], w_down, b_down[None, :],
        g_down[None, :], heads, b_head[None, :], *tables,
    )
    return pl.pallas_call(
        spread_kernel,
        out_shape=jax.ShapeDtypeStruct((own_rows, 256), jnp.bfloat16),
        in_specs=[vmem] * 4,
        out_specs=vmem,
        scratch_shapes=[
            pltpu.VMEM((n, held_rows, 256), jnp.bfloat16),
            pltpu.SemaphoreType.DMA((n,)),
            pltpu.SemaphoreType.DMA((n,)),
        ],
        compiler_params=pltpu.CompilerParams(
            collective_id=0, has_side_effects=True, vmem_limit_bytes=32 * 1024 * 1024
        ),
        name="spread",
    )(encoded, latent_len[None, :], reader[None, :], owner[None, :])


def solution(mesh):
    return jax.shard_map(
        shards,
        mesh=mesh,
        in_specs=(
            P(("groups", "wide"), None),
            P("groups"),
            P("groups"),
            P("groups"),
            P(),
            P(),
            P(),
            P(),
            P(),
            P(),
            P(),
            P(),
        ),
        out_specs=P(("groups", "wide"), None),
        check_vma=False,
    )
```

time: 322 us -> 40.5 us (0.13)
  local copies, waits for them, and re-layouts: 233 us -> 6.35 us
  Pallas kernels: 0 us -> 33.8 us
  matrix products: 23.5 us -> 0 us
  blocking collectives: 21.6 us -> 0 us
  other arithmetic: 17.9 us -> 0 us
  waiting for transfers between devices: 15.3 us -> 0 us
  starting transfers between devices: 7.39 us -> 0 us
    transpose x1, local copies, waits for them, and re-layouts: 101 us -> 1.98 us  [shards(): heads = w_head.reshape(16, 512, 16).transpose(2, 0, 1).reshape(256, 512)]
    slice x5 -> x0, local copies, waits for them, and re-layouts: 44.1 us -> none  [encode_batch(): taps[:, slot:slot + 3].reshape(count, 81, side * side)]
    pallas_call x0 -> x2, Pallas kernels: none -> 33.8 us  [the longest x1 24.1 us: shards(): pl.pallas_call(encode_kernel, out_shape=jax.ShapeDtypeStruct((held_rows,...]
    unnamed x38 -> x32, local copies, waits for them, and re-layouts: 33.1 us -> 0.78 us
    reshape x3 -> x1, local copies, waits for them, and re-layouts: 35.1 us -> 3.59 us  [shards(): heads = w_head.reshape(16, 512, 16).transpose(2, 0, 1).reshape(256, 512)]
    dot_general x4 -> x0, matrix products: 23.5 us -> none  [the longest x1 11.5 us: encode_batch(): jnp.einsum('lm,gmq->glq', w_head, stacked, preferred_element_type=jnp.flo...]
    all_gather x1 -> x0, blocking collectives: 21.6 us -> none  [shards(): shard_rows = lax.all_gather(encoded, 'wide', axis=0, tiled=True)]
    all_to_all x1 -> x0, waiting for transfers between devices: 15.3 us -> none  [shards(): lax.all_to_all(outgoing, 'wide', split_axis=0, concat_axis=0, tiled=True)]
  transfers between devices with their start and end apart: 1 -> 0, of which waited for: 1 -> 0; matrix products, arithmetic and copies ran while one was open for 1% -> 0% of each run, Pallas kernels for 0% -> 0%
where the time goes in v1:
time: 40.5 us; the launch traced here: 40.4 us
  Pallas kernels  33.8 us (83%)
  local copies, waits for them, and re-layouts  6.35 us (16%)
    pallas_call x1, Pallas kernels, shards(): pl.pallas_call(encode_kernel, out_shape=jax.ShapeDtypeStruct((held_rows,...  24.1 us
    pallas_call x1, Pallas kernels, shards(): pl.pallas_call(spread_kernel, out_shape=jax.ShapeDtypeStruct((own_rows, 2...  9.67 us
    reshape x1, local copies, waits for them, and re-layouts, shards(): heads = w_head.reshape(16, 512, 16).transpose(2, 0, 1).reshape(256, 512)  3.59 us
    transpose x1, local copies, waits for them, and re-layouts, shards(): heads = w_head.reshape(16, 512, 16).transpose(2, 0, 1).reshape(256, 512)  1.98 us

profile of v1, /device:TPU:0, one launch (start us, length us, event | category | flops | bytes accessed | tf_op | source)
XLA Modules:
  0.0 40.4 jit_solution(8310091869089563727)
XLA Ops:
  0.0 0.0 copy-start
  0.0 0.0 copy-start.1
  0.0 0.0 copy-start.3
  0.0 0.0 copy-start.5
  0.0 0.0 copy-start.14
  0.0 0.0 copy-start.8
  0.0 0.0 copy-start.9
  0.0 0.0 copy-start.10
  0.0 0.0 copy-start.11
  0.1 0.0 copy-start.12
  0.1 0.0 copy-start.2
  0.1 0.0 copy-start.6
  0.1 0.0 copy-start.7
  0.1 0.0 copy-start.4
  0.1 3.6 %reshape.6 = bf16[16,512,16]{2,1,0:T(8,128)(2,1)} reshape(bf16[16,8192]{1,0:T(8,128)(2,1)} %param.26) | data formatting | bytes 524288 | tf_op jit(solution)/shard_map/reshape | solution.py:273
  3.7 0.0 copy-start.13
  3.7 2.0 %copy.19 = bf16[16,16,512]{2,1,0:T(8,128)(2,1)S(1)} copy(bf16[16,16,512]{0,2,1:T(8,128)(2,1)} %bitcast.19) | data formatting | bytes 524288 | tf_op jit(solution)/shard_map/transpose | solution.py:273
  5.7 0.0 copy-done.14
  5.7 0.1 copy.20.win_ref
  5.8 0.0 copy-done
  5.8 0.0 copy-done.1
  5.8 0.0 copy-done.3
  5.8 0.0 copy-done.5
  5.9 0.0 copy-done.8
  5.9 0.0 copy-done.9
  5.9 0.0 copy-done.10
  5.9 0.0 copy-done.11
  5.9 0.0 copy-done.12
  5.9 0.0 copy-done.2
  5.9 0.0 copy-done.6
  5.9 0.0 copy-done.7
  5.9 0.0 copy-done.4
  5.9 24.1 %encode.1.enc_ref = bf16[16,256]{1,0:T(8,128)(2,1)S(1)} custom-call(s32[32]{0:T(128)S(1)} %copy-done.6, s32[32]{0:T(128)S(1)} %copy-done.7, bf16[64,3072]{1,0:T(8,128)(2,1)S(1)} %copy-done.2, bf16[128,81]{1,0:T(8,128)(2,1)S(1)} %copy.20.win_ref, f32[1,128]{1,0:T(1,128)S(1)} %bitcast.13, f32[1,128]{1,0:T(1,128)S(1)} %bitcast.14, ...), custom_call_target="tpu_custom_call" | custom-call | tf_op jit(solution)/shard_map/encode/pallas_call | solution.py:280
  30.1 0.0 copy-done.13
  30.1 9.7 %spread.1 = bf16[18,256]{1,0:T(8,128)(2,1)S(1)} custom-call(bf16[16,256]{1,0:T(8,128)(2,1)S(1)} %encode.1.enc_ref, s32[1,32]{1,0:T(1,128)S(1)} %bitcast.11, s32[1,32]{1,0:T(1,128)S(1)} %bitcast.12, s32[1,32]{1,0:T(1,128)S(1)} %bitcast.18), custom_call_target="tpu_custom_call" | custom-call | tf_op jit(solution)/shard_map/spread/pallas_call | solution.py:300
  39.8 0.6 %copy.22 = bf16[18,256]{1,0:T(8,128)(2,1)} copy(bf16[18,256]{1,0:T(8,128)(2,1)S(1)} %spread.1) | data formatting | bytes 18432
Async XLA Ops:
  0.0 5.8 %copy-start = (bf16[512,1024]{1,0:T(8,128)(2,1)S(1)}, bf16[512,1024]{1,0:T(8,128)(2,1)}, u32[]{:S(2)}) copy-start(bf16[512,1024]{1,0:T(8,128)(2,1)} %constant.8.clone.wtab_ref) | copy-start | bytes 3145732
  0.0 5.8 %copy-start.1 = (bf16[512,512]{1,0:T(8,128)(2,1)S(1)}, bf16[512,512]{1,0:T(8,128)(2,1)}, u32[]{:S(2)}) copy-start(bf16[512,512]{1,0:T(8,128)(2,1)} %constant.10.clone.dtab_ref) | copy-start | bytes 1572868
  0.0 5.8 %copy-start.3 = (bf16[81,1024]{1,0:T(8,128)(2,1)S(1)}, bf16[81,1024]{1,0:T(8,128)(2,1)}, u32[]{:S(2)}) copy-start(bf16[81,1024]{1,0:T(8,128)(2,1)} %constant.9.clone.etab_ref) | copy-start | bytes 497668
  0.0 5.8 %copy-start.5 = (bf16[256,256]{1,0:T(8,128)(2,1)S(1)}, bf16[256,256]{1,0:T(8,128)(2,1)}, u32[]{:S(2)}) copy-start(bf16[256,256]{1,0:T(8,128)(2,1)} %constant.11.clone.ptab_ref) | copy-start | bytes 393220
  0.0 5.7 %copy-start.14 = (bf16[128,81]{0,1:T(8,128)(2,1)S(1)}, bf16[128,81]{0,1:T(8,128)(2,1)}, u32[]{:S(2)}) copy-start(bf16[128,81]{0,1:T(8,128)(2,1)} %param.20) | copy-start | bytes 62212
  0.0 5.8 %copy-start.8 = (f32[128]{0:T(128)S(1)}, f32[128]{0:T(128)}, u32[]{:S(2)}) copy-start(f32[128]{0:T(128)} %param.21) | copy-start | bytes 1540
  0.0 5.8 %copy-start.9 = (f32[128]{0:T(128)S(1)}, f32[128]{0:T(128)}, u32[]{:S(2)}) copy-start(f32[128]{0:T(128)} %param.22) | copy-start | bytes 1540
  0.0 5.8 %copy-start.10 = (f32[128]{0:T(128)S(1)}, f32[128]{0:T(128)}, u32[]{:S(2)}) copy-start(f32[128]{0:T(128)} %param.24) | copy-start | bytes 1540
  0.0 5.8 %copy-start.11 = (f32[128]{0:T(128)S(1)}, f32[128]{0:T(128)}, u32[]{:S(2)}) copy-start(f32[128]{0:T(128)} %param.25) | copy-start | bytes 1540
  0.1 5.8 %copy-start.12 = (f32[16]{0:T(128)S(1)}, f32[16]{0:T(128)}, u32[]{:S(2)}) copy-start(f32[16]{0:T(128)} %param.27) | copy-start | bytes 196
  0.1 5.8 %copy-start.2 = (bf16[64,3072]{1,0:T(8,128)(2,1)S(1)}, bf16[64,3072]{1,0:T(8,128)(2,1)}, u32[]{:S(2)}) copy-start(bf16[64,3072]{1,0:T(8,128)(2,1)} %frames_ref.1) | copy-start | bytes 1179652
  0.1 5.8 %copy-start.6 = (s32[32]{0:T(128)S(1)}, s32[32]{0:T(128)}, u32[]{:S(2)}) copy-start(s32[32]{0:T(128)} %len_ref.1) | copy-start | bytes 388
  0.1 5.8 %copy-start.7 = (s32[32]{0:T(128)S(1)}, s32[32]{0:T(128)}, u32[]{:S(2)}) copy-start(s32[32]{0:T(128)} %reader_ref.1) | copy-start | bytes 388
  0.1 5.8 %copy-start.4 = (bf16[128,512]{1,0:T(8,128)(2,1)S(1)}, bf16[128,512]{1,0:T(8,128)(2,1)}, u32[]{:S(2)}) copy-start(bf16[128,512]{1,0:T(8,128)(2,1)} %wdown_ref.1) | copy-start | bytes 393220
  3.7 26.4 %copy-start.13 = (s32[32]{0:T(128)S(1)}, s32[32]{0:T(128)}, u32[]{:S(2)}) copy-start(s32[32]{0:T(128)} %param.19) | copy-start | bytes 388

commit v2 on v1

v2 whole, which is shorter than its diff:
```python
import functools

import jax
import jax.numpy as jnp
import numpy as np
from jax import lax
from jax.experimental import pallas as pl
from jax.experimental.pallas import tpu as pltpu
from jax.sharding import PartitionSpec as P

PIX = 32
EPS = 1e-6
WIN = 48
KDIM = 160
HALF = 256
MESH = pl.DeviceIdType.MESH


def window_table():
    table = np.zeros((512, 1024), np.float32)
    for py in range(2):
        for dx in range(4):
            for u in range(8):
                for v in range(16):
                    x = 2 * v + dx - 1
                    if 0 <= x < PIX:
                        table[(2 * u + py) * PIX + x, (py * 4 + dx) * 128 + u * 16 + v] = 1
    return table


def weight_table():
    table = np.zeros((81, 1024), np.float32)
    for py in range(2):
        for px in range(2):
            for t in range(3):
                for a in range(3):
                    for b in range(3):
                        for k in range(3):
                            col = t * WIN + ((a + py) * 4 + b + px) * 3 + k
                            table[t * 27 + (a * 3 + b) * 3 + k, (py * 2 + px) * 256 + col] = 1
    return table


def down_table():
    table = np.zeros((512, 512), np.float32)
    for c in range(128):
        for ab in range(4):
            table[4 * c + ab, ab * 128 + c] = 1
    return table


def place_table():
    px = np.arange(HALF)
    place = (px // 16 // 4) * 4 + (px % 16) // 4
    return (place[:, None] == (np.arange(256) % 16)[None, :]).astype(np.float32)


def head_table():
    table = np.zeros((256, 256), np.float32)
    for j in range(16):
        for ab in range(16):
            table[j * 16 + ab, ab * 16 + j] = 1
    return table


def iota(shape, axis):
    return lax.broadcasted_iota(jnp.int32, shape, axis)


def column(row):
    n = row.shape[1]
    same = iota((n, n), 0) == iota((n, n), 1)
    return jnp.sum(jnp.where(same, row, jnp.zeros((), row.dtype)), axis=1, keepdims=True)


def norm_silu(values, gain):
    mean_square = jnp.sum(values * values, axis=0, keepdims=True) * (1.0 / values.shape[0])
    half = (values * gain) * (0.5 * lax.rsqrt(mean_square + EPS))
    return (half + half * jnp.tanh(half)).astype(jnp.bfloat16)


def norm_silu_packed(values, gain):
    count = values.shape[0]
    packed = values.astype(jnp.bfloat16)
    squares = packed * packed
    while squares.shape[0] > 16:
        middle = squares.shape[0] // 2
        squares = squares[:middle] + squares[middle:]
    mean_square = jnp.sum(squares.astype(jnp.float32), axis=0, keepdims=True) * (1.0 / count)
    scale = (0.5 * lax.rsqrt(mean_square + EPS)).astype(jnp.bfloat16)
    half = (packed * gain) * scale
    return half + half * jnp.tanh(half)


def dot(a, b):
    return jnp.dot(a, b, preferred_element_type=jnp.float32)


def kernel(
    lens_ref, readers_ref, owners_ref, frames_ref, win_ref, bin_ref, gin_ref,
    wdown_ref, bdown_ref, gdown_ref, whead_ref, bhead_ref, wtab_ref, etab_ref, dtab_ref, htab_ref,
    ptab_ref, out_ref, windows, w2, wd, heads, gin_s, gdown_s, bdown_s, parts, flags, enc, held, pick_s,
    send_sem, recv_sem,
):
    me = lax.axis_index("wide")
    n, rows = held.shape[0], held.shape[1]
    barrier = pltpu.get_barrier_semaphore()
    for d in range(1, n):
        pl.semaphore_signal(
            barrier, inc=1, device_id={"wide": lax.rem(me + d, n)}, device_id_type=MESH
        )
    read_rows = frames_ref.shape[0]
    most = read_rows // 4
    clips = lens_ref.shape[1]
    mine_at = me.astype(jnp.float32)
    len_row, reader_row, owner_row = (
        ref[...].astype(jnp.float32) for ref in (lens_ref, readers_ref, owners_ref)
    )
    len_col, reader_col, owner_col = column(len_row), column(reader_row), column(owner_row)
    earlier = iota((clips, clips), 1) < iota((clips, clips), 0)
    before_here = jnp.sum(
        jnp.where(earlier & (reader_row == reader_col), len_row, 0.0), axis=1, keepdims=True
    )
    first_len = jnp.sum(
        jnp.where((reader_col == mine_at) & (before_here == 0.0), len_col, 0.0),
        axis=0,
        keepdims=True,
    )

    last = 4 * most - 6
    row = iota((read_rows, 1), 0)
    number = ((row + 2) // 4 - 1).astype(jnp.float32)
    offset = ((row + 2) % 4).astype(jnp.float32)
    second = jnp.where(number >= first_len - 1.0, 1.0, 0.0)
    step = number + 1.0 - second * (first_len - 1.0)
    second_at = 4.0 * first_len - 3.0
    source = second * second_at + 4.0 * step - 3.0 + offset
    source = jnp.where(row < last, source, -1.0)
    source = jnp.where(row == 0, -1.0, source)
    source = jnp.where(row == 1, 0.0, source)
    source = jnp.where(row == last + 1, second_at, source)
    order = (iota((read_rows, read_rows), 1).astype(jnp.float32) == source).astype(jnp.bfloat16)
    frames = dot(order, frames_ref[...]).astype(jnp.bfloat16)
    flags[...] = jnp.where(
        iota(flags.shape, 0).astype(jnp.float32) == first_len - 1.0, 1.0, 0.0
    ) * jnp.ones(flags.shape, jnp.float32)

    stacked = jnp.concatenate(
        [
            frames[:, k * 1024 + h * 512 : k * 1024 + (h + 1) * 512]
            for k in range(3)
            for h in range(2)
        ],
        axis=0,
    )
    planes = dot(stacked, wtab_ref[...])
    lane = iota((read_rows, HALF), 1)
    for k in range(3):
        for dx in range(4):
            plane = []
            for py in range(2):
                at = (py * 4 + dx) * 128
                plane.append(
                    jnp.concatenate(
                        [
                            planes[
                                (2 * k + h) * read_rows : (2 * k + h + 1) * read_rows,
                                at : at + 128,
                            ]
                            for h in range(2)
                        ],
                        axis=1,
                    )
                )
            above = jnp.where(lane < 16, 0.0, pltpu.roll(plane[1], 16, 1))
            below = jnp.where(lane >= HALF - 16, 0.0, pltpu.roll(plane[0], HALF - 16, 1))
            for dy, value in enumerate((above, plane[0], plane[1], below)):
                row = (dy * 4 + dx) * 3 + k
                for h in range(2):
                    windows[h, pl.ds(row, read_rows, stride=WIN), :] = value[
                        :, h * 128 : (h + 1) * 128
                    ]

    spread = dot(win_ref[...], etab_ref[...])
    bias = column(bin_ref[...])
    high = bias.astype(jnp.bfloat16).astype(jnp.float32)
    mid = (bias - high).astype(jnp.bfloat16).astype(jnp.float32)
    low = bias - high - mid
    kcol = iota((128, KDIM), 1)
    tail = jnp.where(kcol == 3 * WIN, high, 0.0)
    tail = tail + jnp.where(kcol == 3 * WIN + 1, mid, 0.0)
    tail = tail + jnp.where(kcol == 3 * WIN + 2, low, 0.0)
    for ab in range(4):
        w2[ab * 128 : (ab + 1) * 128, :] = (
            spread[:, ab * 256 : ab * 256 + KDIM] + tail
        ).astype(jnp.bfloat16)
    wd[...] = dot(wdown_ref[...], dtab_ref[...]).astype(jnp.bfloat16)
    gin_s[...] = jnp.broadcast_to(column(gin_ref[...]), gin_s.shape).astype(jnp.bfloat16)
    gdown_s[...] = jnp.broadcast_to(column(gdown_ref[...]), gdown_s.shape)
    bdown_s[...] = jnp.broadcast_to(column(bdown_ref[...]), bdown_s.shape)

    chunks = jnp.concatenate(
        [whead_ref[:, (s * 8 + c) * 256 : (s * 8 + c + 1) * 256] for c in range(8) for s in range(4)],
        axis=0,
    )
    turned = dot(chunks, htab_ref[...])
    piece = iota((64, 128), 1) // 16
    for ab in range(16):
        at = ab // 8 * 128
        row = jnp.zeros((64, 128), jnp.float32)
        for c in range(8):
            value = turned[c * 64 : (c + 1) * 64, at : at + 128]
            shift = (16 * c - ab % 8 * 16) % 128
            value = pltpu.roll(value, shift, 1) if shift else value
            row = jnp.where(piece == c, value, row)
        row = row.astype(jnp.bfloat16)
        for s in range(4):
            heads[ab * 16 : (ab + 1) * 16, s * 128 : (s + 1) * 128] = row[s * 16 : (s + 1) * 16]

    own_rows = out_ref.shape[0]
    own_off = jnp.sum(
        jnp.where(earlier & (owner_row == owner_col), len_row, 0.0), axis=1, keepdims=True
    )
    slot = iota((clips, 128), 1).astype(jnp.float32)
    place = slot - own_off
    inside = (owner_col == mine_at) & (place >= 0.0) & (place < len_col)
    late = before_here > 0.0
    opening = jnp.where(late, 1.0, 0.0)
    later = jnp.where(late, before_here, 1.0) + place
    source = reader_col * rows + jnp.where(place == 0.0, opening, later)
    picked = jnp.sum(jnp.where(inside, source + 1.0, 0.0), axis=0, keepdims=True) - 1.0
    pick = (iota((n * rows, 128), 0).astype(jnp.float32) == picked).astype(jnp.float32)
    pick_s[...] = pick.T.astype(jnp.bfloat16)

    ones = jnp.ones((KDIM - 3 * WIN, HALF), jnp.bfloat16)

    def load(slot, count):
        at = pl.multiple_of(slot * WIN, 8)
        halves = [windows[h, pl.ds(at, count * WIN), :] for h in range(2)]
        return jnp.concatenate(halves, axis=1)

    def encode_frame(cols):
        cols = jnp.concatenate([cols, ones], axis=0)
        full = [
            norm_silu_packed(dot(w2[ab * 128 : (ab + 1) * 128, :], cols), gin_s[...]) for ab in range(4)
        ]
        lowered = dot(wd[...], jnp.concatenate(full, axis=0)) + bdown_s[...]
        return norm_silu(lowered, gdown_s[...])

    pix = iota((16, HALF), 1)
    sub = ((pix // 16) % 4) * 4 + pix % 4

    def keep(spot, both):
        total = jnp.zeros((16, HALF), jnp.float32)
        for ab in range(16):
            total = total + jnp.where(sub == ab, both[ab * 16 : (ab + 1) * 16, :], 0.0)
        parts[pl.ds(pl.multiple_of(spot * 16, 16), 16), :] = total

    for spot, at in enumerate((1, last + 1)):
        cols = load(at, 1).astype(jnp.bfloat16)
        cols = jnp.concatenate([jnp.zeros((2 * WIN, HALF), jnp.bfloat16), cols], axis=0)
        keep(spot, dot(heads[:, 384:512], encode_frame(cols)))

    def group(at, carry):
        flag = flags[pl.ds(at, 1), :]
        before = load(4 * at, 2) * (1.0 - flag) + load(last, 2) * flag
        cols = jnp.concatenate([before, load(4 * at + 2, 4)], axis=0).astype(jnp.bfloat16)
        reduced = jnp.concatenate(
            [encode_frame(cols[s * WIN : (s + 3) * WIN, :]) for s in range(4)], axis=0
        )
        keep(at + 2, dot(heads[...], reduced))
        return carry

    lax.fori_loop(0, most - 2, group, 0)

    value = parts[...]
    top = value.astype(jnp.bfloat16)
    rest = (value - top.astype(jnp.float32)).astype(jnp.bfloat16)
    wide = dot(top, ptab_ref[...]) + dot(rest, ptab_ref[...])
    match = iota((most * 16, 256), 1) // 16 == iota((most * 16, 256), 0) % 16
    wide = jnp.where(match, wide, 0.0).reshape(most, 16, 256)
    bh = jnp.where(
        iota((16, 256), 1) // 16 == iota((16, 256), 0), column(bhead_ref[...]), 0.0
    )
    bh = jnp.sum(bh, axis=0, keepdims=True)
    result = jnp.sum(wide, axis=1) + bh
    if rows > most:
        result = jnp.concatenate([result, jnp.zeros((rows - most, 256), jnp.float32)], axis=0)
    enc[...] = result.astype(jnp.bfloat16)

    pl.semaphore_wait(barrier, n - 1)
    copies = []
    for d in range(1, n):
        copy = pltpu.make_async_remote_copy(
            src_ref=enc,
            dst_ref=held.at[me],
            send_sem=send_sem.at[d],
            recv_sem=recv_sem.at[d],
            device_id={"wide": lax.rem(me + d, n)},
            device_id_type=MESH,
        )
        copy.start()
        copies.append(copy)
    held[me] = enc[...]
    for copy in copies:
        copy.wait()
    result = dot(pick_s[...], held[...].reshape(n * rows, 256))
    out_ref[...] = result[:own_rows].astype(jnp.bfloat16)


def shards(
    frames, latent_len, reader, owner, w_in, b_in, g_in, w_down, b_down, g_down, w_head, b_head
):
    n = lax.axis_size("wide")
    read_rows = frames.shape[0]
    most = read_rows // 4
    held_rows = -(-most // 16) * 16
    own_rows = 2 * ((most + 2) // 2)
    vmem = pl.BlockSpec(memory_space=pltpu.VMEM)
    tables = [
        jnp.asarray(t, dtype=jnp.bfloat16)
        for t in (window_table(), weight_table(), down_table(), head_table(), place_table())
    ]
    return pl.pallas_call(
        kernel,
        out_shape=jax.ShapeDtypeStruct((own_rows, 256), jnp.bfloat16),
        in_specs=[vmem] * 17,
        out_specs=vmem,
        scratch_shapes=[
            pltpu.VMEM((2, read_rows * WIN, 128), jnp.float32),
            pltpu.VMEM((512, KDIM), jnp.bfloat16),
            pltpu.VMEM((128, 512), jnp.bfloat16),
            pltpu.VMEM((256, 512), jnp.bfloat16),
            pltpu.VMEM((128, HALF), jnp.bfloat16),
            pltpu.VMEM((128, HALF), jnp.float32),
            pltpu.VMEM((128, HALF), jnp.float32),
            pltpu.VMEM((most * 16, HALF), jnp.float32),
            pltpu.VMEM((most, HALF), jnp.float32),
            pltpu.VMEM((held_rows, 256), jnp.bfloat16),
            pltpu.VMEM((n, held_rows, 256), jnp.bfloat16),
            pltpu.VMEM((128, n * held_rows), jnp.bfloat16),
            pltpu.SemaphoreType.DMA((n,)),
            pltpu.SemaphoreType.DMA((n,)),
        ],
        compiler_params=pltpu.CompilerParams(
            collective_id=0, has_side_effects=True, vmem_limit_bytes=48 * 1024 * 1024
        ),
        name="encode",
    )(
        latent_len[None, :], reader[None, :], owner[None, :], frames, w_in,
        b_in[None, :], g_in[None, :], w_down, b_down[None, :], g_down[None, :], w_head,
        b_head[None, :], *tables,
    )


def solution(mesh):
    return jax.shard_map(
        shards,
        mesh=mesh,
        in_specs=(
            P(("groups", "wide"), None),
            P("groups"),
            P("groups"),
            P("groups"),
            P(),
            P(),
            P(),
            P(),
            P(),
            P(),
            P(),
            P(),
        ),
        out_specs=P(("groups", "wide"), None),
        check_vma=False,
    )
```

time: 40.5 us -> 42.1 us (1.040)
  local copies, waits for them, and re-layouts: 6.35 us -> 9.4 us
  Pallas kernels: 33.8 us -> 32.2 us
    unnamed x32 -> x34, local copies, waits for them, and re-layouts: 0.78 us -> 9.4 us
    reshape x1 -> x0, local copies, waits for them, and re-layouts: 3.59 us -> none  [shards(): heads = w_head.reshape(16, 512, 16).transpose(2, 0, 1).reshape(256, 512)]
    transpose x1 -> x0, local copies, waits for them, and re-layouts: 1.98 us -> none  [shards(): heads = w_head.reshape(16, 512, 16).transpose(2, 0, 1).reshape(256, 512)]
    pallas_call x2 -> x1, Pallas kernels: 33.8 us -> 32.2 us  [shards(): pl.pallas_call(kernel, out_shape=jax.ShapeDtypeStruct((own_rows, 256), jn...]
where the time goes in v2:
time: 42.1 us; the launch traced here: 41.7 us
  Pallas kernels  32.2 us (76%)
  local copies, waits for them, and re-layouts  9.4 us (22%)
    pallas_call x1, Pallas kernels, shards(): pl.pallas_call(kernel, out_shape=jax.ShapeDtypeStruct((own_rows, 256), jn...  32.2 us
    unnamed x34, local copies, waits for them, and re-layouts  9.4 us

profile of v2, /device:TPU:0, one launch (start us, length us, event | category | flops | bytes accessed | tf_op | source)
XLA Modules:
  0.0 41.7 jit_solution(7092895805323052274)
XLA Ops:
  0.0 0.0 copy-start.8
  0.0 0.0 copy-start.9
  0.0 0.0 copy-start.10
  0.0 0.0 copy-start.11
  0.0 0.0 copy-start.12
  0.0 0.0 copy-start.13
  0.0 0.0 copy-start.14
  0.0 0.0 copy-start.15
  0.0 0.9 %copy.18.win_ref = bf16[128,81]{1,0:T(8,128)(2,1)S(1)} copy(bf16[128,81]{0,1:T(8,128)(2,1)} %param.21) | data formatting | bytes 41472 | tf_op args[4]
  1.0 0.0 copy-done.8
  1.0 0.0 copy-done.9
  1.0 0.0 copy-done.10
  1.0 0.0 copy-done.11
  1.0 0.0 copy-done.12
  1.0 0.0 copy-done.13
  1.0 0.0 copy-done.14
  1.0 0.0 copy-done.15
  1.0 0.0 copy-start
  1.1 1.2 %copy-done = bf16[512,1024]{1,0:T(8,128)(2,1)S(1)} copy-done((bf16[512,1024]{1,0:T(8,128)(2,1)S(1)}, bf16[512,1024]{1,0:T(8,128)(2,1)}, u32[]{:S(2)}) %copy-start) | copy-done | bytes 1048600
  2.3 0.0 copy-start.1
  2.3 1.0 %copy-done.1 = bf16[512,512]{1,0:T(8,128)(2,1)S(1)} copy-done((bf16[512,512]{1,0:T(8,128)(2,1)S(1)}, bf16[512,512]{1,0:T(8,128)(2,1)}, u32[]{:S(2)}) %copy-start.1) | copy-done | bytes 524312
  3.3 0.0 copy-start.2
  3.3 1.0 %copy-done.2 = bf16[64,3072]{1,0:T(8,128)(2,1)S(1)} copy-done((bf16[64,3072]{1,0:T(8,128)(2,1)S(1)}, bf16[64,3072]{1,0:T(8,128)(2,1)}, u32[]{:S(2)}) %copy-start.2) | copy-done | bytes 393240
  4.3 0.0 copy-start.3
  4.3 0.9 %copy-done.3 = bf16[16,8192]{1,0:T(8,128)(2,1)S(1)} copy-done((bf16[16,8192]{1,0:T(8,128)(2,1)S(1)}, bf16[16,8192]{1,0:T(8,128)(2,1)}, u32[]{:S(2)}) %copy-start.3) | copy-done | bytes 262168
  5.3 0.0 copy-start.4
  5.3 0.9 %copy-done.4 = bf16[81,1024]{1,0:T(8,128)(2,1)S(1)} copy-done((bf16[81,1024]{1,0:T(8,128)(2,1)S(1)}, bf16[81,1024]{1,0:T(8,128)(2,1)}, u32[]{:S(2)}) %copy-start.4) | copy-done | bytes 165912
  6.2 0.0 copy-start.5
  6.2 0.9 %copy-done.5 = bf16[128,512]{1,0:T(8,128)(2,1)S(1)} copy-done((bf16[128,512]{1,0:T(8,128)(2,1)S(1)}, bf16[128,512]{1,0:T(8,128)(2,1)}, u32[]{:S(2)}) %copy-start.5) | copy-done | bytes 131096
  7.1 0.0 copy-start.6
  7.1 0.9 %copy-done.6 = bf16[256,256]{1,0:T(8,128)(2,1)S(1)} copy-done((bf16[256,256]{1,0:T(8,128)(2,1)S(1)}, bf16[256,256]{1,0:T(8,128)(2,1)}, u32[]{:S(2)}) %copy-start.6) | copy-done | bytes 131096
  8.0 0.0 copy-start.7
  8.0 0.9 %copy-done.7 = bf16[256,256]{1,0:T(8,128)(2,1)S(1)} copy-done((bf16[256,256]{1,0:T(8,128)(2,1)S(1)}, bf16[256,256]{1,0:T(8,128)(2,1)}, u32[]{:S(2)}) %copy-start.7) | copy-done | bytes 131096
  8.9 32.2 %encode.1 = bf16[18,256]{1,0:T(8,128)(2,1)S(1)} custom-call(s32[1,32]{1,0:T(1,128)S(1)} %bitcast.8, s32[1,32]{1,0:T(1,128)S(1)} %bitcast.9, s32[1,32]{1,0:T(1,128)S(1)} %bitcast.10, bf16[64,3072]{1,0:T(8,128)(2,1)S(1)} %copy-done.2, bf16[128,81]{1,0:T(8,128)(2,1)S(1)} %copy.18.win_ref, f32[1,128]{1,0:T(1,128)S(1)} %bitcast.11, f32[1,128]{1,0:T(1,128)S(1)} %bitcast.12, ...), custom_call_target="tpu_custom_call" | custom-call | tf_op jit(solution)/shard_map/encode/pallas_call | solution.py:324
  41.1 0.6 %copy.20 = bf16[18,256]{1,0:T(8,128)(2,1)} copy(bf16[18,256]{1,0:T(8,128)(2,1)S(1)} %encode.1) | data formatting | bytes 18432
Async XLA Ops:
  0.0 1.0 %copy-start.8 = (s32[32]{0:T(128)S(1)}, s32[32]{0:T(128)}, u32[]{:S(2)}) copy-start(s32[32]{0:T(128)} %param.18) | copy-start | bytes 388
  0.0 1.0 %copy-start.9 = (s32[32]{0:T(128)S(1)}, s32[32]{0:T(128)}, u32[]{:S(2)}) copy-start(s32[32]{0:T(128)} %param.19) | copy-start | bytes 388
  0.0 1.0 %copy-start.10 = (s32[32]{0:T(128)S(1)}, s32[32]{0:T(128)}, u32[]{:S(2)}) copy-start(s32[32]{0:T(128)} %param.20) | copy-start | bytes 388
  0.0 1.0 %copy-start.11 = (f32[128]{0:T(128)S(1)}, f32[128]{0:T(128)}, u32[]{:S(2)}) copy-start(f32[128]{0:T(128)} %param.22) | copy-start | bytes 1540
  0.0 1.0 %copy-start.12 = (f32[128]{0:T(128)S(1)}, f32[128]{0:T(128)}, u32[]{:S(2)}) copy-start(f32[128]{0:T(128)} %param.23) | copy-start | bytes 1540
  0.0 1.0 %copy-start.13 = (f32[128]{0:T(128)S(1)}, f32[128]{0:T(128)}, u32[]{:S(2)}) copy-start(f32[128]{0:T(128)} %param.25) | copy-start | bytes 1540
  0.0 1.0 %copy-start.14 = (f32[128]{0:T(128)S(1)}, f32[128]{0:T(128)}, u32[]{:S(2)}) copy-start(f32[128]{0:T(128)} %param.26) | copy-start | bytes 1540
  0.0 1.0 %copy-start.15 = (f32[16]{0:T(128)S(1)}, f32[16]{0:T(128)}, u32[]{:S(2)}) copy-start(f32[16]{0:T(128)} %param.28) | copy-start | bytes 196
  1.0 1.2 %copy-start = (bf16[512,1024]{1,0:T(8,128)(2,1)S(1)}, bf16[512,1024]{1,0:T(8,128)(2,1)}, u32[]{:S(2)}) copy-start(bf16[512,1024]{1,0:T(8,128)(2,1)} %constant.10.clone.wtab_ref) | copy-start | bytes 3145732
  2.3 1.0 %copy-start.1 = (bf16[512,512]{1,0:T(8,128)(2,1)S(1)}, bf16[512,512]{1,0:T(8,128)(2,1)}, u32[]{:S(2)}) copy-start(bf16[512,512]{1,0:T(8,128)(2,1)} %constant.12.clone.dtab_ref) | copy-start | bytes 1572868
  3.3 1.0 %copy-start.2 = (bf16[64,3072]{1,0:T(8,128)(2,1)S(1)}, bf16[64,3072]{1,0:T(8,128)(2,1)}, u32[]{:S(2)}) copy-start(bf16[64,3072]{1,0:T(8,128)(2,1)} %frames_ref.1) | copy-start | bytes 1179652
  4.3 0.9 %copy-start.3 = (bf16[16,8192]{1,0:T(8,128)(2,1)S(1)}, bf16[16,8192]{1,0:T(8,128)(2,1)}, u32[]{:S(2)}) copy-start(bf16[16,8192]{1,0:T(8,128)(2,1)} %whead_ref.1) | copy-start | bytes 786436
  5.3 0.9 %copy-start.4 = (bf16[81,1024]{1,0:T(8,128)(2,1)S(1)}, bf16[81,1024]{1,0:T(8,128)(2,1)}, u32[]{:S(2)}) copy-start(bf16[81,1024]{1,0:T(8,128)(2,1)} %constant.11.clone.etab_ref) | copy-start | bytes 497668
  6.2 0.9 %copy-start.5 = (bf16[128,512]{1,0:T(8,128)(2,1)S(1)}, bf16[128,512]{1,0:T(8,128)(2,1)}, u32[]{:S(2)}) copy-start(bf16[128,512]{1,0:T(8,128)(2,1)} %wdown_ref.1) | copy-start | bytes 393220
  7.1 0.9 %copy-start.6 = (bf16[256,256]{1,0:T(8,128)(2,1)S(1)}, bf16[256,256]{1,0:T(8,128)(2,1)}, u32[]{:S(2)}) copy-start(bf16[256,256]{1,0:T(8,128)(2,1)} %constant.14.clone.ptab_ref) | copy-start | bytes 393220
  8.0 0.9 %copy-start.7 = (bf16[256,256]{1,0:T(8,128)(2,1)S(1)}, bf16[256,256]{1,0:T(8,128)(2,1)}, u32[]{:S(2)}) copy-start(bf16[256,256]{1,0:T(8,128)(2,1)} %constant.13.clone.htab_ref) | copy-start | bytes 393220

commit v3 on v2

--- a/solution.py
+++ b/solution.py
@@ -79,29 +79,26 @@
     return (half + half * jnp.tanh(half)).astype(jnp.bfloat16)
 
 
-def norm_silu_packed(values, gain):
-    count = values.shape[0]
-    packed = values.astype(jnp.bfloat16)
-    squares = packed * packed
-    while squares.shape[0] > 16:
-        middle = squares.shape[0] // 2
-        squares = squares[:middle] + squares[middle:]
-    mean_square = jnp.sum(squares.astype(jnp.float32), axis=0, keepdims=True) * (1.0 / count)
-    scale = (0.5 * lax.rsqrt(mean_square + EPS)).astype(jnp.bfloat16)
-    half = (packed * gain) * scale
-    return half + half * jnp.tanh(half)
-
-
 def dot(a, b):
     return jnp.dot(a, b, preferred_element_type=jnp.float32)
 
 
-def kernel(
-    lens_ref, readers_ref, owners_ref, frames_ref, win_ref, bin_ref, gin_ref,
-    wdown_ref, bdown_ref, gdown_ref, whead_ref, bhead_ref, wtab_ref, etab_ref, dtab_ref, htab_ref,
-    ptab_ref, out_ref, windows, w2, wd, heads, gin_s, gdown_s, bdown_s, parts, flags, enc, held, pick_s,
-    send_sem, recv_sem,
-):
+def kernel(*refs):
+    sources, (out_ref, *rest) = refs[:17], refs[17:]
+    loaded, rest = rest[:17], rest[17:]
+    (windows, w2, wd, heads, gin_s, gdown_s, bdown_s, parts, flags, enc, held, pick_s) = rest[:12]
+    load_sem, send_sem, recv_sem = rest[12:]
+    loads = [
+        pltpu.make_async_copy(source, target, load_sem.at[at])
+        for at, (source, target) in enumerate(zip(sources, loaded))
+    ]
+    for load in loads:
+        load.start()
+    (
+        lens_ref, readers_ref, owners_ref, frames_ref, wtab_ref, win_ref, bin_ref, gin_ref,
+        wdown_ref, bdown_ref, gdown_ref, whead_ref, bhead_ref, etab_ref, dtab_ref, htab_ref,
+        ptab_ref,
+    ) = loaded
     me = lax.axis_index("wide")
     n, rows = held.shape[0], held.shape[1]
     barrier = pltpu.get_barrier_semaphore()
@@ -109,6 +106,8 @@
         pl.semaphore_signal(
             barrier, inc=1, device_id={"wide": lax.rem(me + d, n)}, device_id_type=MESH
         )
+    for load in loads:
+        load.wait()
     read_rows = frames_ref.shape[0]
     most = read_rows // 4
     clips = lens_ref.shape[1]
@@ -181,7 +180,9 @@
                         :, h * 128 : (h + 1) * 128
                     ]
 
-    spread = dot(win_ref[...], etab_ref[...])
+    spread = lax.dot_general(
+        win_ref[...], etab_ref[...], (((0,), (0,)), ((), ())), preferred_element_type=jnp.float32
+    )
     bias = column(bin_ref[...])
     high = bias.astype(jnp.bfloat16).astype(jnp.float32)
     mid = (bias - high).astype(jnp.bfloat16).astype(jnp.float32)
@@ -195,7 +196,7 @@
             spread[:, ab * 256 : ab * 256 + KDIM] + tail
         ).astype(jnp.bfloat16)
     wd[...] = dot(wdown_ref[...], dtab_ref[...]).astype(jnp.bfloat16)
-    gin_s[...] = jnp.broadcast_to(column(gin_ref[...]), gin_s.shape).astype(jnp.bfloat16)
+    gin_s[...] = jnp.broadcast_to(column(gin_ref[...]), gin_s.shape)
     gdown_s[...] = jnp.broadcast_to(column(gdown_ref[...]), gdown_s.shape)
     bdown_s[...] = jnp.broadcast_to(column(bdown_ref[...]), bdown_s.shape)
 
@@ -234,15 +235,16 @@
 
     ones = jnp.ones((KDIM - 3 * WIN, HALF), jnp.bfloat16)
 
-    def load(slot, count):
+    def window(slot, count):
         at = pl.multiple_of(slot * WIN, 8)
         halves = [windows[h, pl.ds(at, count * WIN), :] for h in range(2)]
         return jnp.concatenate(halves, axis=1)
 
     def encode_frame(cols):
         cols = jnp.concatenate([cols, ones], axis=0)
+        convolved = dot(w2[...], cols)
         full = [
-            norm_silu_packed(dot(w2[ab * 128 : (ab + 1) * 128, :], cols), gin_s[...]) for ab in range(4)
+            norm_silu(convolved[ab * 128 : (ab + 1) * 128, :], gin_s[...]) for ab in range(4)
         ]
         lowered = dot(wd[...], jnp.concatenate(full, axis=0)) + bdown_s[...]
         return norm_silu(lowered, gdown_s[...])
@@ -257,14 +259,14 @@
         parts[pl.ds(pl.multiple_of(spot * 16, 16), 16), :] = total
 
     for spot, at in enumerate((1, last + 1)):
-        cols = load(at, 1).astype(jnp.bfloat16)
+        cols = window(at, 1).astype(jnp.bfloat16)
         cols = jnp.concatenate([jnp.zeros((2 * WIN, HALF), jnp.bfloat16), cols], axis=0)
         keep(spot, dot(heads[:, 384:512], encode_frame(cols)))
 
     def group(at, carry):
         flag = flags[pl.ds(at, 1), :]
-        before = load(4 * at, 2) * (1.0 - flag) + load(last, 2) * flag
-        cols = jnp.concatenate([before, load(4 * at + 2, 4)], axis=0).astype(jnp.bfloat16)
+        before = window(4 * at, 2) * (1.0 - flag) + window(last, 2) * flag
+        cols = jnp.concatenate([before, window(4 * at + 2, 4)], axis=0).astype(jnp.bfloat16)
         reduced = jnp.concatenate(
             [encode_frame(cols[s * WIN : (s + 3) * WIN, :]) for s in range(4)], axis=0
         )
@@ -316,22 +318,29 @@
     most = read_rows // 4
     held_rows = -(-most // 16) * 16
     own_rows = 2 * ((most + 2) // 2)
+    hbm = pl.BlockSpec(memory_space=pltpu.HBM)
     vmem = pl.BlockSpec(memory_space=pltpu.VMEM)
-    tables = [
+    wtab, etab, dtab, htab, ptab = (
         jnp.asarray(t, dtype=jnp.bfloat16)
         for t in (window_table(), weight_table(), down_table(), head_table(), place_table())
-    ]
+    )
+    operands = (
+        latent_len[None, :], reader[None, :], owner[None, :], frames, wtab, w_in.T,
+        b_in[None, :], g_in[None, :], w_down, b_down[None, :], g_down[None, :], w_head,
+        b_head[None, :], etab, dtab, htab, ptab,
+    )
     return pl.pallas_call(
         kernel,
         out_shape=jax.ShapeDtypeStruct((own_rows, 256), jnp.bfloat16),
-        in_specs=[vmem] * 17,
+        in_specs=[hbm] * len(operands),
         out_specs=vmem,
-        scratch_shapes=[
+        scratch_shapes=[pltpu.VMEM(value.shape, value.dtype) for value in operands]
+        + [
             pltpu.VMEM((2, read_rows * WIN, 128), jnp.float32),
             pltpu.VMEM((512, KDIM), jnp.bfloat16),
             pltpu.VMEM((128, 512), jnp.bfloat16),
             pltpu.VMEM((256, 512), jnp.bfloat16),
-            pltpu.VMEM((128, HALF), jnp.bfloat16),
+            pltpu.VMEM((128, HALF), jnp.float32),
             pltpu.VMEM((128, HALF), jnp.float32),
             pltpu.VMEM((128, HALF), jnp.float32),
             pltpu.VMEM((most * 16, HALF), jnp.float32),
@@ -339,18 +348,15 @@
             pltpu.VMEM((held_rows, 256), jnp.bfloat16),
             pltpu.VMEM((n, held_rows, 256), jnp.bfloat16),
             pltpu.VMEM((128, n * held_rows), jnp.bfloat16),
+            pltpu.SemaphoreType.DMA((len(operands),)),
             pltpu.SemaphoreType.DMA((n,)),
             pltpu.SemaphoreType.DMA((n,)),
         ],
         compiler_params=pltpu.CompilerParams(
-            collective_id=0, has_side_effects=True, vmem_limit_bytes=48 * 1024 * 1024
+            collective_id=0, has_side_effects=True, vmem_limit_bytes=56 * 1024 * 1024
         ),
         name="encode",
-    )(
-        latent_len[None, :], reader[None, :], owner[None, :], frames, w_in,
-        b_in[None, :], g_in[None, :], w_down, b_down[None, :], g_down[None, :], w_head,
-        b_head[None, :], *tables,
-    )
+    )(*operands)
 
 
 def solution(mesh):

time: 42.1 us -> 39.9 us (0.948)
  local copies, waits for them, and re-layouts: 9.4 us -> 1.31 us
  Pallas kernels: 32.2 us -> 38.3 us
    unnamed x34 -> x1, local copies, waits for them, and re-layouts: 9.4 us -> 1.31 us
    pallas_call x1, Pallas kernels: 32.2 us -> 38.3 us  [shards(): pl.pallas_call(kernel, out_shape=jax.ShapeDtypeStruct((own_rows, 256), jn...]
where the time goes in v3:
time: 39.9 us; the launch traced here: 39.7 us
  Pallas kernels  38.3 us (96%)
  local copies, waits for them, and re-layouts  1.31 us (3%)
    pallas_call x1, Pallas kernels, shards(): pl.pallas_call(kernel, out_shape=jax.ShapeDtypeStruct((own_rows, 256), jn...  38.3 us
    unnamed x1, local copies, waits for them, and re-layouts  1.31 us

profile of v3, /device:TPU:0, one launch (start us, length us, event | category | flops | bytes accessed | tf_op | source)
XLA Modules:
  0.0 39.7 jit_solution(5668148729616111967)
XLA Ops:
  0.0 38.3 %encode.1 = bf16[18,256]{1,0:T(8,128)(2,1)} custom-call(s32[1,32]{1,0:T(1,128)} %bitcast.10, s32[1,32]{1,0:T(1,128)} %bitcast.11, s32[1,32]{1,0:T(1,128)} %bitcast.12, bf16[64,3072]{1,0:T(8,128)(2,1)} %refs_3_.1, bf16[512,1024]{1,0:T(8,128)(2,1)} %constant.10.clone.refs_4_, bf16[81,128]{1,0:T(8,128)(2,1)} %bitcast.9, f32[1,128]{1,0:T(1,128)} %bitcast.13, ...), custom_call_target="tpu_custom_call" | custom-call | tf_op jit(solution)/shard_map/encode/pallas_call | solution.py:332
  38.4 1.3 %copy.19 = bf16[18,256]{1,0:T(8,128)(2,1)} copy(bf16[18,256]{1,0:T(8,128)(2,1)} %encode.1) | data formatting | bytes 18432

commit v4 on v3

--- a/solution.py
+++ b/solution.py
@@ -11,6 +11,7 @@
 PIX = 32
 EPS = 1e-6
 WIN = 48
+PITCH = 49
 KDIM = 160
 HALF = 256
 MESH = pl.DeviceIdType.MESH
@@ -87,7 +88,8 @@
     sources, (out_ref, *rest) = refs[:17], refs[17:]
     loaded, rest = rest[:17], rest[17:]
     (windows, w2, wd, heads, gin_s, gdown_s, bdown_s, parts, flags, enc, held, pick_s) = rest[:12]
-    load_sem, send_sem, recv_sem = rest[12:]
+    convolved, full, reduced = rest[12:15]
+    load_sem, send_sem, recv_sem = rest[15:]
     loads = [
         pltpu.make_async_copy(source, target, load_sem.at[at])
         for at, (source, target) in enumerate(zip(sources, loaded))
@@ -106,7 +108,7 @@
         pl.semaphore_signal(
             barrier, inc=1, device_id={"wide": lax.rem(me + d, n)}, device_id_type=MESH
         )
-    for load in loads:
+    for load in loads[:5]:
         load.wait()
     read_rows = frames_ref.shape[0]
     most = read_rows // 4
@@ -176,10 +178,12 @@
             for dy, value in enumerate((above, plane[0], plane[1], below)):
                 row = (dy * 4 + dx) * 3 + k
                 for h in range(2):
-                    windows[h, pl.ds(row, read_rows, stride=WIN), :] = value[
+                    windows[h, pl.ds(row, read_rows, stride=PITCH), :] = value[
                         :, h * 128 : (h + 1) * 128
                     ]
 
+    for load in loads[5:]:
+        load.wait()
     spread = lax.dot_general(
         win_ref[...], etab_ref[...], (((0,), (0,)), ((), ())), preferred_element_type=jnp.float32
     )
@@ -235,19 +239,26 @@
 
     ones = jnp.ones((KDIM - 3 * WIN, HALF), jnp.bfloat16)
 
-    def window(slot, count):
-        at = pl.multiple_of(slot * WIN, 8)
-        halves = [windows[h, pl.ds(at, count * WIN), :] for h in range(2)]
-        return jnp.concatenate(halves, axis=1)
-
-    def encode_frame(cols):
-        cols = jnp.concatenate([cols, ones], axis=0)
-        convolved = dot(w2[...], cols)
-        full = [
-            norm_silu(convolved[ab * 128 : (ab + 1) * 128, :], gin_s[...]) for ab in range(4)
-        ]
-        lowered = dot(wd[...], jnp.concatenate(full, axis=0)) + bdown_s[...]
-        return norm_silu(lowered, gdown_s[...])
+    def window(slot):
+        return jnp.concatenate(
+            [windows[h, pl.ds(slot * PITCH, WIN), :] for h in range(2)], axis=1
+        )
+
+    def encode_frames(columns_of, count):
+        for t in range(count + 2):
+            cols = jnp.concatenate([columns_of(t), ones], axis=0) if t < count else None
+            for part in range(2):
+                at = part * 256
+                if t < count:
+                    convolved[t % 2, at : at + 256, :] = dot(w2[at : at + 256, :], cols)
+                if 1 <= t <= count:
+                    for row in (at, at + 128):
+                        full[(t - 1) % 2, row : row + 128, :] = norm_silu(
+                            convolved[(t - 1) % 2, row : row + 128, :], gin_s[...]
+                        )
+            if t >= 2:
+                lowered = dot(wd[...], full[t % 2]) + bdown_s[...]
+                reduced[(t - 2) * 128 : (t - 1) * 128, :] = norm_silu(lowered, gdown_s[...])
 
     pix = iota((16, HALF), 1)
     sub = ((pix // 16) % 4) * 4 + pix % 4
@@ -258,22 +269,38 @@
             total = total + jnp.where(sub == ab, both[ab * 16 : (ab + 1) * 16, :], 0.0)
         parts[pl.ds(pl.multiple_of(spot * 16, 16), 16), :] = total
 
-    for spot, at in enumerate((1, last + 1)):
-        cols = window(at, 1).astype(jnp.bfloat16)
-        cols = jnp.concatenate([jnp.zeros((2 * WIN, HALF), jnp.bfloat16), cols], axis=0)
-        keep(spot, dot(heads[:, 384:512], encode_frame(cols)))
-
-    def group(at, carry):
-        flag = flags[pl.ds(at, 1), :]
-        before = window(4 * at, 2) * (1.0 - flag) + window(last, 2) * flag
-        cols = jnp.concatenate([before, window(4 * at + 2, 4)], axis=0).astype(jnp.bfloat16)
-        reduced = jnp.concatenate(
-            [encode_frame(cols[s * WIN : (s + 3) * WIN, :]) for s in range(4)], axis=0
-        )
-        keep(at + 2, dot(heads[...], reduced))
+    blank = jnp.zeros((2 * WIN, HALF), jnp.bfloat16)
+    openings = (1, last + 1)
+    encode_frames(
+        lambda t: jnp.concatenate([blank, window(openings[t]).astype(jnp.bfloat16)], axis=0), 2
+    )
+    for spot in range(2):
+        keep(spot, dot(heads[:, 384:512], reduced[spot * 128 : (spot + 1) * 128, :]))
+
+    pair = 2 if most % 2 == 0 else 1
+
+    def groups(at, carry):
+        made = {}
+
+        def columns_of(t):
+            g = t // 4
+            if g not in made:
+                number = at * pair + g
+                flag = flags[pl.ds(number, 1), :]
+                slots = [
+                    window(4 * number + s) * (1.0 - flag) + window(last + s) * flag
+                    for s in range(2)
+                ]
+                slots += [window(4 * number + s) for s in range(2, 6)]
+                made[g] = jnp.concatenate(slots, axis=0).astype(jnp.bfloat16)
+            return made[g][t % 4 * WIN : (t % 4 + 3) * WIN, :]
+
+        encode_frames(columns_of, 4 * pair)
+        for g in range(pair):
+            keep(at * pair + g + 2, dot(heads[...], reduced[g * 512 : (g + 1) * 512, :]))
         return carry
 
-    lax.fori_loop(0, most - 2, group, 0)
+    lax.fori_loop(0, (most - 2) // pair, groups, 0)
 
     value = parts[...]
     top = value.astype(jnp.bfloat16)
@@ -336,7 +363,7 @@
         out_specs=vmem,
         scratch_shapes=[pltpu.VMEM(value.shape, value.dtype) for value in operands]
         + [
-            pltpu.VMEM((2, read_rows * WIN, 128), jnp.float32),
+            pltpu.VMEM((2, read_rows * PITCH, 128), jnp.float32),
             pltpu.VMEM((512, KDIM), jnp.bfloat16),
             pltpu.VMEM((128, 512), jnp.bfloat16),
             pltpu.VMEM((256, 512), jnp.bfloat16),
@@ -348,12 +375,15 @@
             pltpu.VMEM((held_rows, 256), jnp.bfloat16),
             pltpu.VMEM((n, held_rows, 256), jnp.bfloat16),
             pltpu.VMEM((128, n * held_rows), jnp.bfloat16),
+            pltpu.VMEM((2, 512, HALF), jnp.float32),
+            pltpu.VMEM((2, 512, HALF), jnp.bfloat16),
+            pltpu.VMEM((1024, HALF), jnp.bfloat16),
             pltpu.SemaphoreType.DMA((len(operands),)),
             pltpu.SemaphoreType.DMA((n,)),
             pltpu.SemaphoreType.DMA((n,)),
         ],
         compiler_params=pltpu.CompilerParams(
-            collective_id=0, has_side_effects=True, vmem_limit_bytes=56 * 1024 * 1024
+            collective_id=0, has_side_effects=True, vmem_limit_bytes=32 * 1024 * 1024
         ),
         name="encode",
     )(*operands)

time: 39.9 us -> 37.7 us (0.945)
  Pallas kernels: 38.3 us -> 27.3 us
  local copies, waits for them, and re-layouts: 1.31 us -> 9.91 us
    pallas_call x1, Pallas kernels: 38.3 us -> 27.3 us  [shards(): pl.pallas_call(kernel, out_shape=jax.ShapeDtypeStruct((own_rows, 256), jn...]
    unnamed x1 -> x35, local copies, waits for them, and re-layouts: 1.31 us -> 9.91 us
where the time goes in v4:
time: 37.7 us; the launch traced here: 37.2 us
  Pallas kernels  27.3 us (72%)
  local copies, waits for them, and re-layouts  9.91 us (26%)
    pallas_call x1, Pallas kernels, shards(): pl.pallas_call(kernel, out_shape=jax.ShapeDtypeStruct((own_rows, 256), jn...  27.3 us
    unnamed x35, local copies, waits for them, and re-layouts  9.91 us

profile of v4, /device:TPU:0, one launch (start us, length us, event | category | flops | bytes accessed | tf_op | source)
XLA Modules:
  0.0 37.2 jit_solution(1303904992055628652)
XLA Ops:
  0.0 0.0 copy-start.16
  0.0 0.0 copy-start.12
  0.0 0.0 copy-start.13
  0.0 0.0 copy-start.14
  0.0 0.0 copy-start.15
  0.0 0.0 copy-start.9
  0.0 0.0 copy-start.10
  0.0 0.0 copy-start.11
  0.0 0.6 %copy-done.16 = f32[16]{0:T(128)S(1)} copy-done((f32[16]{0:T(128)S(1)}, f32[16]{0:T(128)}, u32[]{:S(2)}) %copy-start.16) | copy-done | bytes 88
  0.7 0.0 copy-done.12
  0.7 0.0 copy-done.13
  0.7 0.0 copy-done.14
  0.7 0.0 copy-done.15
  0.7 0.0 copy-done.9
  0.7 0.0 copy-done.10
  0.8 0.0 copy-done.11
  0.8 0.0 copy-start
  0.8 1.2 %copy-done = bf16[512,1024]{1,0:T(8,128)(2,1)S(1)} copy-done((bf16[512,1024]{1,0:T(8,128)(2,1)S(1)}, bf16[512,1024]{1,0:T(8,128)(2,1)}, u32[]{:S(2)}) %copy-start) | copy-done | bytes 1048600
  2.0 0.0 copy-start.1
  2.0 1.0 %copy-done.1 = bf16[512,512]{1,0:T(8,128)(2,1)S(1)} copy-done((bf16[512,512]{1,0:T(8,128)(2,1)S(1)}, bf16[512,512]{1,0:T(8,128)(2,1)}, u32[]{:S(2)}) %copy-start.1) | copy-done | bytes 524312
  3.0 0.0 copy-start.2
  3.0 1.0 %copy-done.2 = bf16[64,3072]{1,0:T(8,128)(2,1)S(1)} copy-done((bf16[64,3072]{1,0:T(8,128)(2,1)S(1)}, bf16[64,3072]{1,0:T(8,128)(2,1)}, u32[]{:S(2)}) %copy-start.2) | copy-done | bytes 393240
  4.0 0.0 copy-start.3
  4.0 0.9 %copy-done.3 = bf16[16,8192]{1,0:T(8,128)(2,1)S(1)} copy-done((bf16[16,8192]{1,0:T(8,128)(2,1)S(1)}, bf16[16,8192]{1,0:T(8,128)(2,1)}, u32[]{:S(2)}) %copy-start.3) | copy-done | bytes 262168
  5.0 0.0 copy-start.4
  5.0 0.9 %copy-done.4 = bf16[81,1024]{1,0:T(8,128)(2,1)S(1)} copy-done((bf16[81,1024]{1,0:T(8,128)(2,1)S(1)}, bf16[81,1024]{1,0:T(8,128)(2,1)}, u32[]{:S(2)}) %copy-start.4) | copy-done | bytes 165912
  5.9 0.0 copy-start.5
  5.9 0.9 %copy-done.5 = bf16[128,512]{1,0:T(8,128)(2,1)S(1)} copy-done((bf16[128,512]{1,0:T(8,128)(2,1)S(1)}, bf16[128,512]{1,0:T(8,128)(2,1)}, u32[]{:S(2)}) %copy-start.5) | copy-done | bytes 131096
  6.8 0.0 copy-start.6
  6.8 0.9 %copy-done.6 = bf16[256,256]{1,0:T(8,128)(2,1)S(1)} copy-done((bf16[256,256]{1,0:T(8,128)(2,1)S(1)}, bf16[256,256]{1,0:T(8,128)(2,1)}, u32[]{:S(2)}) %copy-start.6) | copy-done | bytes 131096
  7.7 0.0 copy-start.7
  7.7 0.9 %copy-done.7 = bf16[256,256]{1,0:T(8,128)(2,1)S(1)} copy-done((bf16[256,256]{1,0:T(8,128)(2,1)S(1)}, bf16[256,256]{1,0:T(8,128)(2,1)}, u32[]{:S(2)}) %copy-start.7) | copy-done | bytes 131096
  8.6 0.0 copy-start.8
  8.6 0.7 %copy-done.8 = bf16[128,81]{0,1:T(8,128)(2,1)S(1)} copy-done((bf16[128,81]{0,1:T(8,128)(2,1)S(1)}, bf16[128,81]{0,1:T(8,128)(2,1)}, u32[]{:S(2)}) %copy-start.8) | copy-done | bytes 20760
  9.4 27.3 %encode.1 = bf16[18,256]{1,0:T(8,128)(2,1)S(1)} custom-call(s32[1,32]{1,0:T(1,128)S(1)} %bitcast.10, s32[1,32]{1,0:T(1,128)S(1)} %bitcast.11, s32[1,32]{1,0:T(1,128)S(1)} %bitcast.12, bf16[64,3072]{1,0:T(8,128)(2,1)S(1)} %copy-done.2, bf16[512,1024]{1,0:T(8,128)(2,1)S(1)} %copy-done, bf16[81,128]{1,0:T(8,128)(2,1)S(1)} %bitcast.9, f32[1,128]{1,0:T(1,128)S(1)} %bitcast.13, ...), custom_call_target="tpu_custom_call" | custom-call | tf_op jit(solution)/shard_map/encode/pallas_call | solution.py:359
  36.6 0.6 %copy.19 = bf16[18,256]{1,0:T(8,128)(2,1)} copy(bf16[18,256]{1,0:T(8,128)(2,1)S(1)} %encode.1) | data formatting | bytes 18432
Async XLA Ops:
  0.0 0.7 %copy-start.16 = (f32[16]{0:T(128)S(1)}, f32[16]{0:T(128)}, u32[]{:S(2)}) copy-start(f32[16]{0:T(128)} %param.28) | copy-start | bytes 196
  0.0 0.7 %copy-start.12 = (f32[128]{0:T(128)S(1)}, f32[128]{0:T(128)}, u32[]{:S(2)}) copy-start(f32[128]{0:T(128)} %param.22) | copy-start | bytes 1540
  0.0 0.7 %copy-start.13 = (f32[128]{0:T(128)S(1)}, f32[128]{0:T(128)}, u32[]{:S(2)}) copy-start(f32[128]{0:T(128)} %param.23) | copy-start | bytes 1540
  0.0 0.7 %copy-start.14 = (f32[128]{0:T(128)S(1)}, f32[128]{0:T(128)}, u32[]{:S(2)}) copy-start(f32[128]{0:T(128)} %param.25) | copy-start | bytes 1540
  0.0 0.7 %copy-start.15 = (f32[128]{0:T(128)S(1)}, f32[128]{0:T(128)}, u32[]{:S(2)}) copy-start(f32[128]{0:T(128)} %param.26) | copy-start | bytes 1540
  0.0 0.7 %copy-start.9 = (s32[32]{0:T(128)S(1)}, s32[32]{0:T(128)}, u32[]{:S(2)}) copy-start(s32[32]{0:T(128)} %param.18) | copy-start | bytes 388
  0.0 0.7 %copy-start.10 = (s32[32]{0:T(128)S(1)}, s32[32]{0:T(128)}, u32[]{:S(2)}) copy-start(s32[32]{0:T(128)} %param.19) | copy-start | bytes 388
  0.0 0.7 %copy-start.11 = (s32[32]{0:T(128)S(1)}, s32[32]{0:T(128)}, u32[]{:S(2)}) copy-start(s32[32]{0:T(128)} %param.20) | copy-start | bytes 388
  0.8 1.2 %copy-start = (bf16[512,1024]{1,0:T(8,128)(2,1)S(1)}, bf16[512,1024]{1,0:T(8,128)(2,1)}, u32[]{:S(2)}) copy-start(bf16[512,1024]{1,0:T(8,128)(2,1)} %constant.10.clone.refs_4_) | copy-start | bytes 3145732
  2.0 1.0 %copy-start.1 = (bf16[512,512]{1,0:T(8,128)(2,1)S(1)}, bf16[512,512]{1,0:T(8,128)(2,1)}, u32[]{:S(2)}) copy-start(bf16[512,512]{1,0:T(8,128)(2,1)} %constant.12.clone.refs_14_) | copy-start | bytes 1572868
  3.0 1.0 %copy-start.2 = (bf16[64,3072]{1,0:T(8,128)(2,1)S(1)}, bf16[64,3072]{1,0:T(8,128)(2,1)}, u32[]{:S(2)}) copy-start(bf16[64,3072]{1,0:T(8,128)(2,1)} %refs_3_.1) | copy-start | bytes 1179652
  4.0 0.9 %copy-start.3 = (bf16[16,8192]{1,0:T(8,128)(2,1)S(1)}, bf16[16,8192]{1,0:T(8,128)(2,1)}, u32[]{:S(2)}) copy-start(bf16[16,8192]{1,0:T(8,128)(2,1)} %refs_11_.1) | copy-start | bytes 786436
  5.0 0.9 %copy-start.4 = (bf16[81,1024]{1,0:T(8,128)(2,1)S(1)}, bf16[81,1024]{1,0:T(8,128)(2,1)}, u32[]{:S(2)}) copy-start(bf16[81,1024]{1,0:T(8,128)(2,1)} %constant.11.clone.refs_13_) | copy-start | bytes 497668
  5.9 0.9 %copy-start.5 = (bf16[128,512]{1,0:T(8,128)(2,1)S(1)}, bf16[128,512]{1,0:T(8,128)(2,1)}, u32[]{:S(2)}) copy-start(bf16[128,512]{1,0:T(8,128)(2,1)} %refs_8_.1) | copy-start | bytes 393220
  6.8 0.9 %copy-start.6 = (bf16[256,256]{1,0:T(8,128)(2,1)S(1)}, bf16[256,256]{1,0:T(8,128)(2,1)}, u32[]{:S(2)}) copy-start(bf16[256,256]{1,0:T(8,128)(2,1)} %constant.14.clone.refs_16_) | copy-start | bytes 393220
  7.7 0.9 %copy-start.7 = (bf16[256,256]{1,0:T(8,128)(2,1)S(1)}, bf16[256,256]{1,0:T(8,128)(2,1)}, u32[]{:S(2)}) copy-start(bf16[256,256]{1,0:T(8,128)(2,1)} %constant.13.clone.refs_15_) | copy-start | bytes 393220
  8.6 0.7 %copy-start.8 = (bf16[128,81]{0,1:T(8,128)(2,1)S(1)}, bf16[128,81]{0,1:T(8,128)(2,1)}, u32[]{:S(2)}) copy-start(bf16[128,81]{0,1:T(8,128)(2,1)} %param.21) | copy-start | bytes 62212

commit v5 on v3

--- a/solution.py
+++ b/solution.py
@@ -11,6 +11,7 @@
 PIX = 32
 EPS = 1e-6
 WIN = 48
+PITCH = 49
 KDIM = 160
 HALF = 256
 MESH = pl.DeviceIdType.MESH
@@ -87,7 +88,8 @@
     sources, (out_ref, *rest) = refs[:17], refs[17:]
     loaded, rest = rest[:17], rest[17:]
     (windows, w2, wd, heads, gin_s, gdown_s, bdown_s, parts, flags, enc, held, pick_s) = rest[:12]
-    load_sem, send_sem, recv_sem = rest[12:]
+    convolved, full, reduced = rest[12:15]
+    load_sem, send_sem, recv_sem = rest[15:]
     loads = [
         pltpu.make_async_copy(source, target, load_sem.at[at])
         for at, (source, target) in enumerate(zip(sources, loaded))
@@ -106,7 +108,7 @@
         pl.semaphore_signal(
             barrier, inc=1, device_id={"wide": lax.rem(me + d, n)}, device_id_type=MESH
         )
-    for load in loads:
+    for load in loads[:5]:
         load.wait()
     read_rows = frames_ref.shape[0]
     most = read_rows // 4
@@ -176,10 +178,12 @@
             for dy, value in enumerate((above, plane[0], plane[1], below)):
                 row = (dy * 4 + dx) * 3 + k
                 for h in range(2):
-                    windows[h, pl.ds(row, read_rows, stride=WIN), :] = value[
+                    windows[h, pl.ds(row, read_rows, stride=PITCH), :] = value[
                         :, h * 128 : (h + 1) * 128
                     ]
 
+    for load in loads[5:]:
+        load.wait()
     spread = lax.dot_general(
         win_ref[...], etab_ref[...], (((0,), (0,)), ((), ())), preferred_element_type=jnp.float32
     )
@@ -235,19 +239,28 @@
 
     ones = jnp.ones((KDIM - 3 * WIN, HALF), jnp.bfloat16)
 
-    def window(slot, count):
-        at = pl.multiple_of(slot * WIN, 8)
-        halves = [windows[h, pl.ds(at, count * WIN), :] for h in range(2)]
-        return jnp.concatenate(halves, axis=1)
-
-    def encode_frame(cols):
-        cols = jnp.concatenate([cols, ones], axis=0)
-        convolved = dot(w2[...], cols)
-        full = [
-            norm_silu(convolved[ab * 128 : (ab + 1) * 128, :], gin_s[...]) for ab in range(4)
-        ]
-        lowered = dot(wd[...], jnp.concatenate(full, axis=0)) + bdown_s[...]
-        return norm_silu(lowered, gdown_s[...])
+    def window(slot):
+        return jnp.concatenate(
+            [windows[h, pl.ds(slot * PITCH, WIN), :] for h in range(2)], axis=1
+        )
+
+    def stage(cols, odd, spot):
+        if cols is not None:
+            cols = jnp.concatenate([cols, ones], axis=0)
+        for part in range(2):
+            at = part * 256
+            if cols is not None:
+                convolved[odd, at : at + 256, :] = dot(w2[at : at + 256, :], cols)
+            for row in (at, at + 128):
+                full[1 - odd, row : row + 128, :] = norm_silu(
+                    convolved[1 - odd, row : row + 128, :], gin_s[...]
+                )
+        if spot is not None:
+            second_product(odd, spot)
+
+    def second_product(odd, spot):
+        lowered = dot(wd[...], full[odd]) + bdown_s[...]
+        reduced[spot * 128 : (spot + 1) * 128, :] = norm_silu(lowered, gdown_s[...])
 
     pix = iota((16, HALF), 1)
     sub = ((pix // 16) % 4) * 4 + pix % 4
@@ -258,22 +271,43 @@
             total = total + jnp.where(sub == ab, both[ab * 16 : (ab + 1) * 16, :], 0.0)
         parts[pl.ds(pl.multiple_of(spot * 16, 16), 16), :] = total
 
-    for spot, at in enumerate((1, last + 1)):
-        cols = window(at, 1).astype(jnp.bfloat16)
-        cols = jnp.concatenate([jnp.zeros((2 * WIN, HALF), jnp.bfloat16), cols], axis=0)
-        keep(spot, dot(heads[:, 384:512], encode_frame(cols)))
+    def opening(at):
+        blank = jnp.zeros((2 * WIN, HALF), jnp.bfloat16)
+        return jnp.concatenate([blank, window(at).astype(jnp.bfloat16)], axis=0)
+
+    def group_columns(at):
+        flag = flags[pl.ds(at, 1), :]
+        slots = [
+            window(4 * at + s) * (1.0 - flag) + window(last + s) * flag for s in range(2)
+        ]
+        slots += [window(4 * at + s) for s in range(2, 6)]
+        cols = jnp.concatenate(slots, axis=0).astype(jnp.bfloat16)
+        return [cols[s * WIN : (s + 3) * WIN, :] for s in range(4)]
+
+    first = jnp.concatenate([opening(1), ones], axis=0)
+    convolved[0] = dot(w2[...], first)
+    stage(opening(last + 1), 1, None)
+    cols = group_columns(0)
+    stage(cols[0], 0, 2)
+    keep(0, dot(heads[:, 384:512], reduced[256:384, :]))
+    stage(cols[1], 1, 3)
+    keep(1, dot(heads[:, 384:512], reduced[384:512, :]))
+    stage(cols[2], 0, 0)
+    stage(cols[3], 1, 1)
 
     def group(at, carry):
-        flag = flags[pl.ds(at, 1), :]
-        before = window(4 * at, 2) * (1.0 - flag) + window(last, 2) * flag
-        cols = jnp.concatenate([before, window(4 * at + 2, 4)], axis=0).astype(jnp.bfloat16)
-        reduced = jnp.concatenate(
-            [encode_frame(cols[s * WIN : (s + 3) * WIN, :]) for s in range(4)], axis=0
-        )
-        keep(at + 2, dot(heads[...], reduced))
+        cols = group_columns(at)
+        stage(cols[0], 0, 2)
+        stage(cols[1], 1, 3)
+        keep(at + 1, dot(heads[...], reduced[...]))
+        stage(cols[2], 0, 0)
+        stage(cols[3], 1, 1)
         return carry
 
-    lax.fori_loop(0, most - 2, group, 0)
+    lax.fori_loop(1, most - 2, group, 0)
+    stage(None, 0, 2)
+    second_product(1, 3)
+    keep(most - 1, dot(heads[...], reduced[...]))
 
     value = parts[...]
     top = value.astype(jnp.bfloat16)
@@ -336,7 +370,7 @@
         out_specs=vmem,
         scratch_shapes=[pltpu.VMEM(value.shape, value.dtype) for value in operands]
         + [
-            pltpu.VMEM((2, read_rows * WIN, 128), jnp.float32),
+            pltpu.VMEM((2, read_rows * PITCH, 128), jnp.float32),
             pltpu.VMEM((512, KDIM), jnp.bfloat16),
             pltpu.VMEM((128, 512), jnp.bfloat16),
             pltpu.VMEM((256, 512), jnp.bfloat16),
@@ -348,6 +382,9 @@
             pltpu.VMEM((held_rows, 256), jnp.bfloat16),
             pltpu.VMEM((n, held_rows, 256), jnp.bfloat16),
             pltpu.VMEM((128, n * held_rows), jnp.bfloat16),
+            pltpu.VMEM((2, 512, HALF), jnp.float32),
+            pltpu.VMEM((2, 512, HALF), jnp.bfloat16),
+            pltpu.VMEM((512, HALF), jnp.bfloat16),
             pltpu.SemaphoreType.DMA((len(operands),)),
             pltpu.SemaphoreType.DMA((n,)),
             pltpu.SemaphoreType.DMA((n,)),

time: 39.9 us -> 29.3 us (0.73)
  Pallas kernels: 38.3 us -> 27.7 us
    pallas_call x1, Pallas kernels: 38.3 us -> 27.7 us  [shards(): pl.pallas_call(kernel, out_shape=jax.ShapeDtypeStruct((own_rows, 256), jn...]
where the time goes in v5:
time: 29.3 us; the launch traced here: 29.1 us
  Pallas kernels  27.7 us (95%)
  local copies, waits for them, and re-layouts  1.31 us (4%)
    pallas_call x1, Pallas kernels, shards(): pl.pallas_call(kernel, out_shape=jax.ShapeDtypeStruct((own_rows, 256), jn...  27.7 us
    unnamed x1, local copies, waits for them, and re-layouts  1.31 us

profile of v5, /device:TPU:0, one launch (start us, length us, event | category | flops | bytes accessed | tf_op | source)
XLA Modules:
  0.0 29.1 jit_solution(3340242283906540883)
XLA Ops:
  0.0 27.7 %encode.1 = bf16[18,256]{1,0:T(8,128)(2,1)} custom-call(s32[1,32]{1,0:T(1,128)} %bitcast.10, s32[1,32]{1,0:T(1,128)} %bitcast.11, s32[1,32]{1,0:T(1,128)} %bitcast.12, bf16[64,3072]{1,0:T(8,128)(2,1)} %refs_3_.1, bf16[512,1024]{1,0:T(8,128)(2,1)} %constant.10.clone.refs_4_, bf16[81,128]{1,0:T(8,128)(2,1)} %bitcast.9, f32[1,128]{1,0:T(1,128)} %bitcast.13, ...), custom_call_target="tpu_custom_call" | custom-call | tf_op jit(solution)/shard_map/encode/pallas_call | solution.py:366
  27.8 1.3 %copy.19 = bf16[18,256]{1,0:T(8,128)(2,1)} copy(bf16[18,256]{1,0:T(8,128)(2,1)} %encode.1) | data formatting | bytes 18432

commit v6 on v5

--- a/solution.py
+++ b/solution.py
@@ -222,7 +222,6 @@
         for s in range(4):
             heads[ab * 16 : (ab + 1) * 16, s * 128 : (s + 1) * 128] = row[s * 16 : (s + 1) * 16]
 
-    own_rows = out_ref.shape[0]
     own_off = jnp.sum(
         jnp.where(earlier & (owner_row == owner_col), len_row, 0.0), axis=1, keepdims=True
     )
@@ -246,15 +245,11 @@
 
     def stage(cols, odd, spot):
         if cols is not None:
-            cols = jnp.concatenate([cols, ones], axis=0)
-        for part in range(2):
-            at = part * 256
-            if cols is not None:
-                convolved[odd, at : at + 256, :] = dot(w2[at : at + 256, :], cols)
-            for row in (at, at + 128):
-                full[1 - odd, row : row + 128, :] = norm_silu(
-                    convolved[1 - odd, row : row + 128, :], gin_s[...]
-                )
+            convolved[odd] = dot(w2[...], jnp.concatenate([cols, ones], axis=0))
+        for row in range(0, 512, 128):
+            full[1 - odd, row : row + 128, :] = norm_silu(
+                convolved[1 - odd, row : row + 128, :], gin_s[...]
+            )
         if spot is not None:
             second_product(odd, spot)
 
@@ -341,7 +336,7 @@
     for copy in copies:
         copy.wait()
     result = dot(pick_s[...], held[...].reshape(n * rows, 256))
-    out_ref[...] = result[:own_rows].astype(jnp.bfloat16)
+    out_ref[...] = result[: out_ref.shape[0]]
 
 
 def shards(
@@ -363,9 +358,9 @@
         b_in[None, :], g_in[None, :], w_down, b_down[None, :], g_down[None, :], w_head,
         b_head[None, :], etab, dtab, htab, ptab,
     )
-    return pl.pallas_call(
+    picked = pl.pallas_call(
         kernel,
-        out_shape=jax.ShapeDtypeStruct((own_rows, 256), jnp.bfloat16),
+        out_shape=jax.ShapeDtypeStruct((-(-own_rows // 8) * 8, 256), jnp.float32),
         in_specs=[hbm] * len(operands),
         out_specs=vmem,
         scratch_shapes=[pltpu.VMEM(value.shape, value.dtype) for value in operands]
@@ -394,6 +389,7 @@
         ),
         name="encode",
     )(*operands)
+    return picked[:own_rows].astype(jnp.bfloat16)
 
 
 def solution(mesh):

time: 29.3 us -> 28.9 us (0.986)
  Pallas kernels: 27.7 us -> 27.4 us
    slice x0 -> x1, local copies, waits for them, and re-layouts: none -> 1.34 us  [shards(): return picked[:own_rows].astype(jnp.bfloat16)]
    unnamed x1 -> x0, local copies, waits for them, and re-layouts: 1.31 us -> none
    pallas_call x1, Pallas kernels: 27.7 us -> 27.4 us  [shards(): pl.pallas_call(kernel, out_shape=jax.ShapeDtypeStruct((-(-own_rows // 8)...]
where the time goes in v6:
time: 28.9 us; the launch traced here: 28.7 us
  Pallas kernels  27.4 us (95%)
  local copies, waits for them, and re-layouts  1.34 us (5%)
    pallas_call x1, Pallas kernels, shards(): pl.pallas_call(kernel, out_shape=jax.ShapeDtypeStruct((-(-own_rows // 8)...  27.4 us
    slice x1, local copies, waits for them, and re-layouts, shards(): return picked[:own_rows].astype(jnp.bfloat16)  1.34 us

profile of v6, /device:TPU:0, one launch (start us, length us, event | category | flops | bytes accessed | tf_op | source)
XLA Modules:
  0.0 28.7 jit_solution(7960872233114093737)
XLA Ops:
  0.0 27.4 %encode.1 = f32[24,256]{1,0:T(8,128)} custom-call(s32[1,32]{1,0:T(1,128)} %bitcast.10, s32[1,32]{1,0:T(1,128)} %bitcast.11, s32[1,32]{1,0:T(1,128)} %bitcast.12, bf16[64,3072]{1,0:T(8,128)(2,1)} %refs_3_.1, bf16[512,1024]{1,0:T(8,128)(2,1)} %constant.10.clone.refs_4_, bf16[81,128]{1,0:T(8,128)(2,1)} %bitcast.9, f32[1,128]{1,0:T(1,128)} %bitcast.13, ...), custom_call_target="tpu_custom_call" | custom-call | tf_op jit(solution)/shard_map/encode/pallas_call | solution.py:361
  27.4 1.3 %slice.7 = bf16[18,256]{1,0:T(8,128)(2,1)} slice(f32[24,256]{1,0:T(8,128)} %encode.1), slice={[0:18], [0:256]} | slice | bytes 18432 | tf_op jit(solution)/shard_map/slice | solution.py:392

commit v7 on v6

--- a/solution.py
+++ b/solution.py
@@ -108,7 +108,7 @@
         pl.semaphore_signal(
             barrier, inc=1, device_id={"wide": lax.rem(me + d, n)}, device_id_type=MESH
         )
-    for load in loads[:5]:
+    for load in loads[:4]:
         load.wait()
     read_rows = frames_ref.shape[0]
     most = read_rows // 4
@@ -154,6 +154,7 @@
         ],
         axis=0,
     )
+    loads[4].wait()
     planes = dot(stacked, wtab_ref[...])
     lane = iota((read_rows, HALF), 1)
     for k in range(3):
@@ -299,7 +300,13 @@
         stage(cols[3], 1, 1)
         return carry
 
-    lax.fori_loop(1, most - 2, group, 0)
+    def pair(at, carry):
+        group(2 * at + 1, carry)
+        return group(2 * at + 2, carry)
+
+    lax.fori_loop(0, (most - 3) // 2, pair, 0)
+    if most % 2 == 0:
+        group(most - 3, 0)
     stage(None, 0, 2)
     second_product(1, 3)
     keep(most - 1, dot(heads[...], reduced[...]))

time: 28.9 us -> 27.9 us (0.965)
  Pallas kernels: 27.4 us -> 26.3 us
    pallas_call x1, Pallas kernels: 27.4 us -> 26.3 us  [shards(): pl.pallas_call(kernel, out_shape=jax.ShapeDtypeStruct((-(-own_rows // 8)...]
where the time goes in v7:
time: 27.9 us; the launch traced here: 27.7 us
  Pallas kernels  26.3 us (94%)
  local copies, waits for them, and re-layouts  1.34 us (5%)
    pallas_call x1, Pallas kernels, shards(): pl.pallas_call(kernel, out_shape=jax.ShapeDtypeStruct((-(-own_rows // 8)...  26.3 us
    slice x1, local copies, waits for them, and re-layouts, shards(): return picked[:own_rows].astype(jnp.bfloat16)  1.34 us

profile of v7, /device:TPU:0, one launch (start us, length us, event | category | flops | bytes accessed | tf_op | source)
XLA Modules:
  0.0 27.7 jit_solution(7196782421037212870)
XLA Ops:
  0.0 26.3 %encode.1 = f32[24,256]{1,0:T(8,128)} custom-call(s32[1,32]{1,0:T(1,128)} %bitcast.10, s32[1,32]{1,0:T(1,128)} %bitcast.11, s32[1,32]{1,0:T(1,128)} %bitcast.12, bf16[64,3072]{1,0:T(8,128)(2,1)} %refs_3_.1, bf16[512,1024]{1,0:T(8,128)(2,1)} %constant.10.clone.refs_4_, bf16[81,128]{1,0:T(8,128)(2,1)} %bitcast.9, f32[1,128]{1,0:T(1,128)} %bitcast.13, ...), custom_call_target="tpu_custom_call" | custom-call | tf_op jit(solution)/shard_map/encode/pallas_call | solution.py:368
  26.3 1.3 %slice.7 = bf16[18,256]{1,0:T(8,128)(2,1)} slice(f32[24,256]{1,0:T(8,128)} %encode.1), slice={[0:18], [0:256]} | slice | bytes 18432 | tf_op jit(solution)/shard_map/slice | solution.py:399
